TPU v7x, 128 devices: a whole 4x4x4 slice. The times are simulated.
128 devices in a mesh: tm: 4 (over y), height: 8 (over x_lo, z), seq: 4 (over x_hi, core).
Axes of the slice: x: 4 (x_hi: 2, x_lo: 2; x = x_hi * 2 + x_lo), y: 4, z: 4, core: 2. Of those that a mesh axis runs over, the one named last changes fastest.
Arguments:
- latents: float32 [1, 16, 16, 32, 64], P(None, 'tm', None, ('height', 'seq')), may hold values from -8 to 8
- w_in: float32 [3, 3, 3, 16, 384], replicated, may hold values from -0.3125 to 0.3125
- b_in: float32 [384], replicated, may hold values from -1.8 to 1.8
- norm_gain: float32 [384], replicated, may hold values from 0.1 to 1.9
- norm_shift: float32 [384], replicated, may hold values from -1.8 to 1.8
- w_mid: float32 [3, 3, 3, 384, 384], replicated, may hold values from -0.0625 to 0.0625
- b_mid: float32 [384], replicated, may hold values from -1.8 to 1.8
- w_time: float32 [3, 384, 768], replicated, may hold values from -0.1875 to 0.1875
- b_time: float32 [768], replicated, may hold values from -1.8 to 1.8
- w_up: float32 [3, 3, 384, 192], replicated, may hold values from -0.109375 to 0.109375
- b_up: float32 [192], replicated, may hold values from -1.8 to 1.8
Outputs:
- decoded: float32 [1, 32, 64, 128, 192], P(None, ('tm', 'seq'), 'height')
All inputs are finite; a program needn't handle non-finite values.
Results may differ from a plain program's by a relative error of at most 0.0001.
Values sent between devices are 32-bit elements; how exact they have to be, the bound alone decides.
No kernel may reach another device: no remote copies, remote signals or barrier semaphores. Data moves between devices by JAX's collectives and lax.ppermute only.
A program may use at most 128 MiB of HBM per device.

v0:
```python
import jax
import jax.numpy as jnp
from jax import lax
from jax.experimental import pallas as pl
from jax.experimental.pallas import tpu as pltpu
from jax.sharding import PartitionSpec as P

EPS = 1e-06
F32 = jnp.float32
BF16 = jnp.bfloat16
AXES = ("tm", "height", "seq")
VMEM = pl.BlockSpec(memory_space=pltpu.VMEM)
ANY = pl.BlockSpec(memory_space=pl.ANY)


def split(value):
    hi = value.astype(BF16)
    return hi, (value - hi.astype(F32)).astype(BF16)


def dot(a, b):
    return jnp.dot(a, b, preferred_element_type=F32)


def dot_rows(a, b):
    return lax.dot_general(a, b, (((0,), (0,)), ((), ())), preferred_element_type=F32)


def send(value, target):
    n_tm, n_height, n_seq = (lax.axis_size(axis) for axis in AXES)
    place = lambda t, h, s: (t * n_height + h) * n_seq + s
    pairs = []
    for t in range(n_tm):
        for h in range(n_height):
            for s in range(n_seq):
                end = target(t, h, s)
                if end is not None and 0 <= end[0] < n_tm and 0 <= end[1] < n_height:
                    pairs.append((place(t, h, s), place(*end)))
    return lax.ppermute(value, AXES, pairs)


def blend_kernel(
    up_ref, mid_ref, down_ref, w_in_ref, b_in_ref, gain_ref, shift_ref, b_mid_ref, w_mid_ref,
    own_ref, send_ref,
    raw, taps_hi, taps_lo, start, inner_hi, inner_lo, w_hi, w_lo, acc, sems,
):
    for slot, lag in enumerate((0, 2, 1)):
        pltpu.make_async_copy(w_mid_ref.at[lag], raw.at[lag], sems.at[lag]).start()

    t, h, s = (lax.axis_index(axis) for axis in AXES)
    core = lax.rem(s, 2)
    first = 4 * t + 2 * lax.div(s, 2) + 2 * core - 4

    lat = jnp.concatenate(
        [ref[j] for ref in (up_ref, mid_ref, down_ref) for j in range(2)], axis=1
    )
    col = lax.broadcasted_iota(jnp.int32, (1, 512), 1) % 64
    for down in range(3):
        for side in range(3):
            offset = 64 * (1 + down) + side - 1
            piece = pltpu.roll(lat, 768 - offset, 1)[:, :512]
            if side == 0:
                piece = jnp.where(col == 0, 0.0, piece)
            if side == 2:
                piece = jnp.where(col == 63, 0.0, piece)
            hi, lo = split(piece)
            for f in range(6):
                at = f * 144 + (down * 3 + side) * 16
                taps_hi[at : at + 16, :] = hi[f * 16 : f * 16 + 16]
                taps_lo[at : at + 16, :] = lo[f * 16 : f * 16 + 16]

    win_hi, win_lo = split(w_in_ref[...])
    row = lax.broadcasted_iota(jnp.int32, (512, 1), 0) // 64 + (4 * h - 2)
    row_ok = jnp.logical_and(row >= 0, row < 32)
    hidden = []
    for f in range(4):
        x_hi = taps_hi[f * 144 : f * 144 + 432, :]
        x_lo = taps_lo[f * 144 : f * 144 + 432, :]
        init = dot_rows(x_hi, win_hi) + dot_rows(x_lo, win_hi) + dot_rows(x_hi, win_lo)
        init = init + b_in_ref[...]
        if f >= 2:
            start[f - 2] = init[64:448]
        mean_square = jnp.mean(init * init, axis=-1, keepdims=True)
        value = init / jnp.sqrt(mean_square + EPS) * gain_ref[...] + shift_ref[...]
        value = value / (1.0 + jnp.exp(-value))
        hidden.append(jnp.where(jnp.logical_and(row_ok, first + f >= 0), value, 0.0))

    d0, d1, d2, d3 = hidden
    for p, value in enumerate((d0 - d2, d1 - d3, d1 + d2, d2 - d1)):
        hi, lo = split(value)
        for down in range(3):
            inner_hi[p, :, down * 384 : down * 384 + 384] = hi[down * 64 : down * 64 + 384]
            inner_lo[p, :, down * 384 : down * 384 + 384] = lo[down * 64 : down * 64 + 384]

    for p in range(4):
        if p < 3:
            lag = (0, 2, 1)[p]
            pltpu.make_async_copy(w_mid_ref.at[lag], raw.at[lag], sems.at[lag]).wait()
        for down in range(3):
            for side in range(3):
                if p == 0:
                    w = raw[0, down, side]
                elif p == 1:
                    w = raw[2, down, side]
                else:
                    even = 0.5 * (raw[0, down, side] + raw[2, down, side])
                    odd = 0.5 * raw[1, down, side]
                    w = even + odd if p == 2 else even - odd
                hi, lo = split(w)
                at = (p % 2, slice(down * 384, down * 384 + 384), slice(side * 384, side * 384 + 384))
                w_hi[at] = hi
                w_lo[at] = lo
        b_hi, b_lo = w_hi[p % 2], w_lo[p % 2]
        y = dot(inner_hi[p], b_hi) + dot(inner_lo[p], b_hi) + dot(inner_hi[p], b_lo)
        if p == 0:
            acc[0] = y
        elif p == 1:
            acc[1] = -y
        elif p == 2:
            acc[0] += y
            acc[1] += y
        else:
            acc[0] += y
            acc[1] -= y

    place = lax.broadcasted_iota(jnp.int32, (384, 1), 0) % 64
    for j in range(2):
        left = jnp.where(place == 0, 0.0, pltpu.roll(acc[j, :, 0:384], 1, 0))
        right = jnp.where(place == 63, 0.0, pltpu.roll(acc[j, :, 768:1152], 383, 0))
        out = start[j] + b_mid_ref[...] + left + acc[j, :, 384:768] + right
        own_ref[j] = jnp.where(first + 2 + j >= 0, out, 0.0)
    send_ref[...] = own_ref[1 - core]


def upsample_kernel(
    own_ref, got_ref, w_time_ref, b_time_ref, w_up_ref, b_up_ref,
    out_ref,
    hist_hi, hist_lo, x_hi, x_lo, d_hi, d_lo, mixed,
):
    h, s = lax.axis_index("height"), lax.axis_index("seq")
    even_core = lax.rem(s, 2) == 0
    own0, own1, got = own_ref[0], own_ref[1], got_ref[...]
    frames = (
        jnp.where(even_core, own0, got),
        jnp.where(even_core, own1, own0),
        jnp.where(even_core, got, own1),
    )
    for lag, value in enumerate(frames):
        hist_hi[:, lag * 384 : lag * 384 + 384], hist_lo[:, lag * 384 : lag * 384 + 384] = split(value)
    t_hi, t_lo = split(w_time_ref[...])
    paired = dot(hist_hi[...], t_hi) + dot(hist_lo[...], t_hi) + dot(hist_hi[...], t_lo)
    row = lax.broadcasted_iota(jnp.int32, (384, 1), 0) // 64 + (4 * h - 1)
    paired = jnp.where(jnp.logical_and(row >= 0, row < 32), paired + b_time_ref[...], 0.0)

    place = lax.broadcasted_iota(jnp.int32, (384, 1), 0) % 64
    for f in range(2):
        x = paired[:, f * 384 : f * 384 + 384]
        left = jnp.where(place == 0, 0.0, pltpu.roll(x, 1, 0))
        right = jnp.where(place == 63, 0.0, pltpu.roll(x, 383, 0))
        for c, value in enumerate((left, x, right)):
            lanes = slice(c * 384, c * 384 + 384)
            x_hi[f, :, lanes], x_lo[f, :, lanes] = split(value[64:320])
            d_hi[f, :, lanes], d_lo[f, :, lanes] = split(value[0:320] - value[64:384])

    b_up = jnp.concatenate([b_up_ref[...], jnp.zeros((1, 64), F32)], axis=1)
    for b in range(2):
        weights = []
        for sel in ((0,), (0, 1, 2), (2,)):
            cols = [sum(w_up_ref[r, c] for r in sel) for c in range(3)]
            parts = (cols[0], cols[1] + cols[2]) if b == 0 else (cols[0] + cols[1], cols[2])
            both = jnp.concatenate(parts, axis=0)
            weights.append(split(jnp.concatenate([both, jnp.zeros((768, 64), F32)], axis=1)))
        lanes = slice(b * 384, b * 384 + 768)
        for f in range(2):
            def product(hi, lo, w):
                return dot(hi, w[0]) + dot(lo, w[0]) + dot(hi, w[1])

            m1 = product(d_hi[f, 0:256, lanes], d_lo[f, 0:256, lanes], weights[0])
            m2 = product(x_hi[f, :, lanes], x_lo[f, :, lanes], weights[1]) + b_up
            m3 = product(d_hi[f, 64:320, lanes], d_lo[f, 64:320, lanes], weights[2])
            for a, value in enumerate((m1 + m2, m2 - m3)):
                for i in range(4):
                    for j in range(2):
                        mixed[f, 2 * i + a, j, pl.ds(b, 64, stride=2), :] = value[
                            i * 64 : i * 64 + 64, j * 128 : j * 128 + 128
                        ]
    out_ref[:, :, :, 0:128] = mixed[:, :, 0]
    out_ref[:, :, :, 128:192] = mixed[:, :, 1, :, 0:64]


def gather_latents(latents):
    s = lax.axis_index("seq")
    core, half = s % 2, s // 2
    row = latents[0, :, :, 0, :]
    other = send(row, lambda t, h, s: (t, h, s ^ 1))
    pair = jnp.where(
        core == 0, jnp.concatenate([row, other], axis=-1), jnp.concatenate([other, row], axis=-1)
    )
    other = send(pair, lambda t, h, s: (t, h, s ^ 2))
    slab = jnp.where(half == 0, jnp.stack([pair, other]), jnp.stack([other, pair]))
    before = send(slab, lambda t, h, s: (t + 2 if s == 0 else t + 1, h, s))
    beside = send(before, lambda t, h, s: (t, h, 0) if s == 1 else None)
    frames = jnp.where(
        s == 0,
        jnp.concatenate([before[:, 2:], beside], axis=1),
        jnp.where(
            s == 3,
            jnp.concatenate([before[:, 2:], slab], axis=1),
            jnp.concatenate([before, slab[:, :2]], axis=1),
        ),
    ).reshape(2, 96, 128)
    up = send(frames, lambda t, h, s: (t, h + 1, s))
    down = send(frames, lambda t, h, s: (t, h - 1, s))
    return up, frames, down


def body(latents, w_in, b_in, norm_gain, norm_shift, w_mid, b_mid, w_time, b_time, w_up, b_up):
    up, frames, down = gather_latents(latents)
    own, outgoing = pl.pallas_call(
        blend_kernel,
        out_shape=(
            jax.ShapeDtypeStruct((2, 384, 384), F32),
            jax.ShapeDtypeStruct((384, 384), F32),
        ),
        in_specs=[VMEM] * 8 + [ANY],
        out_specs=(VMEM, VMEM),
        scratch_shapes=[
            pltpu.VMEM((3, 3, 3, 384, 384), F32),
            pltpu.VMEM((864, 512), BF16),
            pltpu.VMEM((864, 512), BF16),
            pltpu.VMEM((2, 384, 384), F32),
            pltpu.VMEM((4, 384, 1152), BF16),
            pltpu.VMEM((4, 384, 1152), BF16),
            pltpu.VMEM((2, 1152, 1152), BF16),
            pltpu.VMEM((2, 1152, 1152), BF16),
            pltpu.VMEM((2, 384, 1152), F32),
            pltpu.SemaphoreType.DMA((3,)),
        ],
        compiler_params=pltpu.CompilerParams(vmem_limit_bytes=60 << 20),
        name="blend",
    )(
        up, frames, down, w_in.reshape(432, 384), b_in[None], norm_gain[None], norm_shift[None],
        b_mid[None], w_mid,
    )
    got = send(outgoing, lambda t, h, s: (t, h, s ^ 1))
    out = pl.pallas_call(
        upsample_kernel,
        out_shape=jax.ShapeDtypeStruct((2, 8, 128, 192), F32),
        in_specs=[VMEM] * 6,
        out_specs=VMEM,
        scratch_shapes=[
            pltpu.VMEM((384, 1152), BF16),
            pltpu.VMEM((384, 1152), BF16),
            pltpu.VMEM((2, 256, 1152), BF16),
            pltpu.VMEM((2, 256, 1152), BF16),
            pltpu.VMEM((2, 320, 1152), BF16),
            pltpu.VMEM((2, 320, 1152), BF16),
            pltpu.VMEM((2, 8, 2, 128, 128), F32),
        ],
        compiler_params=pltpu.CompilerParams(vmem_limit_bytes=60 << 20),
        name="upsample",
    )(own, got, w_time.reshape(1152, 768), b_time[None], w_up, b_up[None])
    return out[None]


def solution(mesh):
    placed = (P(None, "tm", None, ("height", "seq"), None),) + (P(),) * 10
    return jax.shard_map(
        body,
        mesh=mesh,
        in_specs=placed,
        out_specs=P(None, ("tm", "seq"), "height", None, None),
        check_vma=False,
    )
```

profile of v0, /device:TPU:27, one launch (start us, length us, event | category | flops | bytes accessed | tf_op | source)
XLA Modules:
  0.0 80.3 jit_solution(2584558823477664516)
XLA Ops:
  0.0 0.7 collective-permute-start
  0.7 1.1 %collective-permute-done = f32[4,16,64]{2,1,0:T(8,128)S(1)} collective-permute-done((f32[4,16,64]{2,1,0:T(8,128)}, f32[4,16,64]{2,1,0:T(8,128)S(1)}, u32[]{:S(2)}, u32[]{:S(2)}) %collective-permute-start) | collective-permute-done | bytes 16416 | tf_op jit(solution)/shard_map/ppermute | solution.py:39
  1.7 0.9 %maximum_select_fusion.2 = f32[4,16,128]{2,1,0:T(8,128)S(1)} fusion(f32[4,16,64]{2,1,0:T(8,128)S(1)} %collective-permute-done, f32[4,16,64]{2,1,0:T(8,128)} %bitcast.16, pred[]{:T(512)S(6)} %eq.16), kind=kLoop, calls=%fused_computation.6 | loop fusion | flops 24576 | bytes 65537 | tf_op jit(solution)/shard_map/jit(_where)/select_n | solution.py:196
  2.7 1.9 %collective-permute-start.1 = (f32[4,16,128]{2,1,0:T(8,128)S(1)}, f32[4,16,128]{2,1,0:T(8,128)S(1)}, u32[]{:S(2)}, u32[]{:S(2)}) collective-permute-start(f32[4,16,128]{2,1,0:T(8,128)S(1)} %maximum_select_fusion.2), channel_id=1, source_target_pairs={{0,2},{1,3},{2,0},{3,1},{4,6},{5,7},{6,4},{7,5},{8,10},{9,11},{10,... | collective-permute-start | bytes 98312 | tf_op jit(solution)/shard_map/ppermute | solution.py:39
  4.6 0.9 %maximum_select_fusion.1 = f32[1,4,16,128]{3,2,1,0:T(8,128)S(1)} fusion(f32[1,4,16,64]{3,2,1,0:T(8,128)S(1)} %bitcast.18, f32[1,4,16,64]{3,2,1,0:T(8,128)} %bitcast.17, pred[]{:T(512)S(6)} %eq.16), kind=kLoop, calls=%fused_computation.5 | loop fusion | flops 24576 | bytes 65537 | tf_op jit(solution)/shard_map/jit(_where)/select_n | solution.py:196
  5.5 1.5 %collective-permute-done.1 = f32[4,16,128]{2,1,0:T(8,128)S(1)} collective-permute-done((f32[4,16,128]{2,1,0:T(8,128)S(1)}, f32[4,16,128]{2,1,0:T(8,128)S(1)}, u32[]{:S(2)}, u32[]{:S(2)}) %collective-permute-start.1) | collective-permute-done | bytes 32800 | tf_op jit(solution)/shard_map/ppermute | solution.py:39
  7.0 1.3 %collective-permute-start.2 = (f32[2,4,16,128]{3,2,1,0:T(8,128)S(1)}, f32[2,4,16,128]{3,2,1,0:T(8,128)S(1)}, u32[]{:S(2)}, u32[]{:S(2)}) collective-permute-start(f32[2,4,16,128]{3,2,1,0:T(8,128)S(1)} %maximum_select_fusion), channel_id=1, source_target_pairs={{0,64},{1,33},{2,34},{3,35},{4,68},{5,37},{6,38},{7,39},{8,72},{9,... | collective-permute-start | bytes 196616 | tf_op jit(solution)/shard_map/ppermute | solution.py:39
  8.3 3.7 %collective-permute-done.2 = f32[2,4,16,128]{3,2,1,0:T(8,128)S(1)} collective-permute-done((f32[2,4,16,128]{3,2,1,0:T(8,128)S(1)}, f32[2,4,16,128]{3,2,1,0:T(8,128)S(1)}, u32[]{:S(2)}, u32[]{:S(2)}) %collective-permute-start.2) | collective-permute-done | bytes 65568 | tf_op jit(solution)/shard_map/ppermute | solution.py:39
  12.0 6.0 %collective-permute-start.3 = (f32[2,4,16,128]{3,2,1,0:T(8,128)S(1)}, f32[2,4,16,128]{3,2,1,0:T(8,128)S(1)}, u32[]{:S(2)}, u32[]{:S(2)}) collective-permute-start(f32[2,4,16,128]{3,2,1,0:T(8,128)S(1)} %collective-permute-done.2), channel_id=1, source_target_pairs={{1,0},{5,4},{9,8},{13,12},{17,16},{21,20},{25,24},{29,28},{33,32},... | collective-permute-start | bytes 196616 | tf_op jit(solution)/shard_map/ppermute | solution.py:39
  18.1 0.8 %collective-permute-done.3 = f32[2,4,16,128]{3,2,1,0:T(8,128)S(1)} collective-permute-done((f32[2,4,16,128]{3,2,1,0:T(8,128)S(1)}, f32[2,4,16,128]{3,2,1,0:T(8,128)S(1)}, u32[]{:S(2)}, u32[]{:S(2)}) %collective-permute-start.3) | collective-permute-done | bytes 65568 | tf_op jit(solution)/shard_map/ppermute | solution.py:39
  19.0 0.0 copy-start.2
  19.0 5.6 %collective-permute-start.5 = (f32[2,96,128]{2,1,0:T(8,128)S(1)}, f32[2,96,128]{2,1,0:T(8,128)S(1)}, u32[]{:S(2)}, u32[]{:S(2)}) collective-permute-start(f32[2,96,128]{2,1,0:T(8,128)S(1)} %bitcast.12), channel_id=1, source_target_pairs={{4,0},{5,1},{6,2},{7,3},{8,4},{9,5},{10,6},{11,7},{12,8},{13,9},{1... | collective-permute-start | bytes 294920 | tf_op jit(solution)/shard_map/ppermute | solution.py:39
  24.7 1.9 %collective-permute-start.4 = (f32[2,96,128]{2,1,0:T(8,128)S(1)}, f32[2,96,128]{2,1,0:T(8,128)S(1)}, u32[]{:S(2)}, u32[]{:S(2)}) collective-permute-start(f32[2,96,128]{2,1,0:T(8,128)S(1)} %bitcast.13), channel_id=1, source_target_pairs={{0,4},{1,5},{2,6},{3,7},{4,8},{5,9},{6,10},{7,11},{8,12},{9,13},{1... | collective-permute-start | bytes 294920 | tf_op jit(solution)/shard_map/ppermute | solution.py:39
  26.6 1.3 %broadcast_in_dim.21.b_in_ref = f32[1,384]{1,0:T(1,128)} reshape(f32[384]{0:T(512)} %param.13) | data formatting | bytes 3072 | tf_op jit(solution)/shard_map/broadcast_in_dim | solution.py:242
  27.9 1.3 %broadcast_in_dim.22.gain_ref = f32[1,384]{1,0:T(1,128)} reshape(f32[384]{0:T(512)} %param.14) | data formatting | bytes 3072 | tf_op jit(solution)/shard_map/broadcast_in_dim | solution.py:242
  29.1 1.3 %broadcast_in_dim.23.shift_ref = f32[1,384]{1,0:T(1,128)} reshape(f32[384]{0:T(512)} %param.15) | data formatting | bytes 3072 | tf_op jit(solution)/shard_map/broadcast_in_dim | solution.py:242
  30.4 1.2 %broadcast_in_dim.24.b_mid_ref = f32[1,384]{1,0:T(1,128)} reshape(f32[384]{0:T(512)} %param.17) | data formatting | bytes 3072 | tf_op jit(solution)/shard_map/broadcast_in_dim | solution.py:243
  31.6 0.0 collective-permute-done.5.down_ref
  31.6 0.0 copy-start.3
  31.6 0.5 collective-permute-done.4.up_ref
  32.1 0.0 copy-start.4
  32.1 0.0 copy-done.2
  32.1 0.1 copy-done.3
  32.2 0.5 copy-done.4
  32.7 0.0 copy-start.5
  32.8 0.0 copy-start
  32.8 25.7 %blend.1 = (f32[2,384,384]{2,1,0:T(8,128)}, f32[384,384]{1,0:T(8,128)}) custom-call(f32[2,96,128]{2,1,0:T(8,128)} %copy-done.4, f32[2,96,128]{2,1,0:T(8,128)} %bitcast.14, f32[2,96,128]{2,1,0:T(8,128)} %copy-done.3, f32[432,384]{1,0:T(8,128)} %bitcast.11, f32[1,384]{1,0:T(1,128)} %broadcast_in_dim.21.b_in_ref, f32[1,384]{1,0:T(1,128)} %broadcast_in_dim.22.gain_ref, ...), custom_call_target="tpu_custom_call" | custom-call | tf_op jit(solution)/shard_map/blend/pallas_call | solution.py:219
  58.5 2.1 %collective-permute-start.6 = (f32[384,384]{1,0:T(8,128)}, f32[384,384]{1,0:T(8,128)S(1)}, u32[]{:S(2)}, u32[]{:S(2)}) collective-permute-start(f32[384,384]{1,0:T(8,128)} %get-tuple-element.8), channel_id=1, source_target_pairs={{0,1},{1,0},{2,3},{3,2},{4,5},{5,4},{6,7},{7,6},{8,9},{9,8},{10,11... | collective-permute-start | bytes 1769480 | tf_op jit(solution)/shard_map/ppermute | solution.py:39
  60.6 0.0 copy-done.5
  60.6 0.6 broadcast_in_dim.25.b_time_ref
  61.2 0.0 copy-done
  61.2 2.9 %copy.12.w_up_ref = f32[3,3,384,192]{3,2,1,0:T(8,128)} copy(f32[3,3,384,192]{2,3,1,0:T(8,128)S(1)} %copy-done) | data formatting | bytes 5308416 | tf_op args[9]
  64.1 0.0 collective-permute-done.6.got_ref
  64.1 0.0 copy-start.1
  64.1 0.8 %copy-done.1 = f32[384,384]{1,0:T(8,128)} copy-done((f32[384,384]{1,0:T(8,128)}, f32[384,384]{1,0:T(8,128)S(1)}, u32[]{:S(2)}) %copy-start.1) | copy-done | bytes 589848
  64.9 12.6 %upsample.1 = f32[2,8,128,192]{3,2,1,0:T(8,128)} custom-call(f32[2,384,384]{2,1,0:T(8,128)} %get-tuple-element.7.own_ref, f32[384,384]{1,0:T(8,128)} %copy-done.1, f32[1152,768]{1,0:T(8,128)} %bitcast.10, f32[1,768]{1,0:T(1,128)} %broadcast_in_dim.25.b_time_ref, f32[3,3,384,192]{3,2,1,0:T(8,128)} %copy.12.w_up_ref, f32[1,192]{1,0:T(1,128)} %bitcast.20), custom_call_target="tpu_custom_call" | custom-call | tf_op jit(solution)/shard_map/upsample/pallas_call | solution.py:246
  77.5 2.8 %copy.13 = f32[1,2,8,128,192]{3,4,2,1,0:T(8,128)} copy(f32[1,2,8,128,192]{4,3,2,1,0:T(8,128)} %bitcast.9) | data formatting | bytes 3145728 | tf_op jit(solution)/shard_map/broadcast_in_dim | solution.py:263
  (4 shorter events, 0.0 us)
Async XLA Ops:
  0.0 1.7 %collective-permute-start = (f32[4,16,64]{2,1,0:T(8,128)}, f32[4,16,64]{2,1,0:T(8,128)S(1)}, u32[]{:S(2)}, u32[]{:S(2)}) collective-permute-start(f32[4,16,64]{2,1,0:T(8,128)} %bitcast.15), channel_id=1, source_target_pairs={{0,1},{1,0},{2,3},{3,2},{4,5},{5,4},{6,7},{7,6},{8,9},{9,8},{10,11... | collective-permute-start | bytes 49160 | tf_op jit(solution)/shard_map/ppermute | solution.py:39
  2.7 4.3 %collective-permute-start.1 = (f32[4,16,128]{2,1,0:T(8,128)S(1)}, f32[4,16,128]{2,1,0:T(8,128)S(1)}, u32[]{:S(2)}, u32[]{:S(2)}) collective-permute-start(f32[4,16,128]{2,1,0:T(8,128)S(1)} %maximum_select_fusion.2), channel_id=1, source_target_pairs={{0,2},{1,3},{2,0},{3,1},{4,6},{5,7},{6,4},{7,5},{8,10},{9,11},{10,... | collective-permute-start | bytes 98312 | tf_op jit(solution)/shard_map/ppermute | solution.py:39
  7.0 5.0 %collective-permute-start.2 = (f32[2,4,16,128]{3,2,1,0:T(8,128)S(1)}, f32[2,4,16,128]{3,2,1,0:T(8,128)S(1)}, u32[]{:S(2)}, u32[]{:S(2)}) collective-permute-start(f32[2,4,16,128]{3,2,1,0:T(8,128)S(1)} %maximum_select_fusion), channel_id=1, source_target_pairs={{0,64},{1,33},{2,34},{3,35},{4,68},{5,37},{6,38},{7,39},{8,72},{9,... | collective-permute-start | bytes 196616 | tf_op jit(solution)/shard_map/ppermute | solution.py:39
  12.0 6.9 %collective-permute-start.3 = (f32[2,4,16,128]{3,2,1,0:T(8,128)S(1)}, f32[2,4,16,128]{3,2,1,0:T(8,128)S(1)}, u32[]{:S(2)}, u32[]{:S(2)}) collective-permute-start(f32[2,4,16,128]{3,2,1,0:T(8,128)S(1)} %collective-permute-done.2), channel_id=1, source_target_pairs={{1,0},{5,4},{9,8},{13,12},{17,16},{21,20},{25,24},{29,28},{33,32},... | collective-permute-start | bytes 196616 | tf_op jit(solution)/shard_map/ppermute | solution.py:39
  19.0 13.1 %copy-start.2 = (f32[2,6,16,128]{3,2,1,0:T(8,128)}, f32[2,6,16,128]{3,2,1,0:T(8,128)S(1)}, u32[]{:S(2)}) copy-start(f32[2,6,16,128]{3,2,1,0:T(8,128)S(1)} %fusion) | copy-start | bytes 294916
  19.0 12.6 %collective-permute-start.5 = (f32[2,96,128]{2,1,0:T(8,128)S(1)}, f32[2,96,128]{2,1,0:T(8,128)S(1)}, u32[]{:S(2)}, u32[]{:S(2)}) collective-permute-start(f32[2,96,128]{2,1,0:T(8,128)S(1)} %bitcast.12), channel_id=1, source_target_pairs={{4,0},{5,1},{6,2},{7,3},{8,4},{9,5},{10,6},{11,7},{12,8},{13,9},{1... | collective-permute-start | bytes 294920 | tf_op jit(solution)/shard_map/ppermute | solution.py:39
  24.7 7.5 %collective-permute-start.4 = (f32[2,96,128]{2,1,0:T(8,128)S(1)}, f32[2,96,128]{2,1,0:T(8,128)S(1)}, u32[]{:S(2)}, u32[]{:S(2)}) collective-permute-start(f32[2,96,128]{2,1,0:T(8,128)S(1)} %bitcast.13), channel_id=1, source_target_pairs={{0,4},{1,5},{2,6},{3,7},{4,8},{5,9},{6,10},{7,11},{8,12},{9,13},{1... | collective-permute-start | bytes 294920 | tf_op jit(solution)/shard_map/ppermute | solution.py:39
  31.6 0.6 copy-start.3
  32.1 0.6 copy-start.4
  32.7 27.8 %copy-start.5 = (f32[768]{0:T(1024)S(1)}, f32[768]{0:T(1024)}, u32[]{:S(2)}) copy-start(f32[768]{0:T(1024)} %param.19) | copy-start | bytes 9220
  32.8 28.4 %copy-start = (f32[3,3,384,192]{2,3,1,0:T(8,128)S(1)}, f32[3,3,384,192]{2,3,1,0:T(8,128)}, u32[]{:S(2)}) copy-start(f32[3,3,384,192]{2,3,1,0:T(8,128)} %param.20) | copy-start | bytes 7962628
  58.5 5.6 %collective-permute-start.6 = (f32[384,384]{1,0:T(8,128)}, f32[384,384]{1,0:T(8,128)S(1)}, u32[]{:S(2)}, u32[]{:S(2)}) collective-permute-start(f32[384,384]{1,0:T(8,128)} %get-tuple-element.8), channel_id=1, source_target_pairs={{0,1},{1,0},{2,3},{3,2},{4,5},{5,4},{6,7},{7,6},{8,9},{9,8},{10,11... | collective-permute-start | bytes 1769480 | tf_op jit(solution)/shard_map/ppermute | solution.py:39
  64.1 0.8 %copy-start.1 = (f32[384,384]{1,0:T(8,128)}, f32[384,384]{1,0:T(8,128)S(1)}, u32[]{:S(2)}) copy-start(f32[384,384]{1,0:T(8,128)S(1)} %collective-permute-done.6.got_ref) | copy-start | bytes 1769476
where the time goes:
time: 80.8 us; the launch traced here: 80.3 us
  Pallas kernels  38.3 us (47%)
  starting transfers between devices  19.6 us (24%)
  local copies, waits for them, and re-layouts  12.8 us (16%)
  waiting for transfers between devices  7.64 us (9%)
  other arithmetic  1.85 us (2%)
    pallas_call x1, Pallas kernels, body(): pl.pallas_call(blend_kernel, out_shape=(jax.ShapeDtypeStruct((2, 384, 384...  25.7 us
    ppermute x7, starting transfers between devices, send(): return lax.ppermute(value, AXES, pairs)  19.6 us
    pallas_call x1, Pallas kernels, body(): pl.pallas_call(upsample_kernel, out_shape=jax.ShapeDtypeStruct((2, 8, 128...  12.6 us
    ppermute x7, waiting for transfers between devices, send(): return lax.ppermute(value, AXES, pairs)  7.64 us
    unnamed x13, local copies, waits for them, and re-layouts  4.39 us
    broadcast_in_dim x1, local copies, waits for them, and re-layouts, body(): return out[None]  2.78 us
    select_n x2, other arithmetic, gather_latents(): jnp.where(core == 0, jnp.concatenate([row, other], axis=-1), jnp.concaten...  1.83 us
  transfers between devices with their start and end apart: 7, of which 5 were waited for; matrix products, arithmetic and copies ran while one was open for 12% of the time, Pallas kernels for 0%

commit v1 on v0

v1 whole, which is shorter than its diff:
```python
import jax
import jax.numpy as jnp
from jax import lax
from jax.experimental import pallas as pl
from jax.experimental.pallas import tpu as pltpu
from jax.sharding import PartitionSpec as P

EPS = 1e-06
F32 = jnp.float32
BF16 = jnp.bfloat16
AXES = ("tm", "height", "seq")
COST = 10_000_000_000
VMEM = pl.BlockSpec(memory_space=pltpu.VMEM)


def dot_lanes(a, b):
    return lax.dot_general(a, b, (((1,), (1,)), ((), ())), preferred_element_type=F32)


def split(value):
    hi = value.astype(BF16)
    return hi, (value - hi.astype(F32)).astype(BF16)


def dot(a, b):
    return jnp.dot(a, b, preferred_element_type=F32)


def dot_rows(a, b):
    return lax.dot_general(a, b, (((0,), (0,)), ((), ())), preferred_element_type=F32)


def send(value, target):
    n_tm, n_height, n_seq = (lax.axis_size(axis) for axis in AXES)
    place = lambda t, h, s: (t * n_height + h) * n_seq + s
    pairs = []
    for t in range(n_tm):
        for h in range(n_height):
            for s in range(n_seq):
                end = target(t, h, s)
                if end is not None and 0 <= end[0] < n_tm and 0 <= end[1] < n_height:
                    pairs.append((place(t, h, s), place(*end)))
    return lax.ppermute(value, AXES, pairs)


def blend_kernel(
    mid_ref, far_ref, near_ref, w_in_ref, b_in_ref, gain_ref, shift_ref, b_mid_ref, raw,
    own_ref, send_ref,
    taps_hi, taps_lo, start, inner, weights, acc,
):
    t, h, s = (lax.axis_index(axis) for axis in AXES)
    core = lax.rem(s, 2)
    first = 4 * t + 2 * lax.div(s, 2) + 2 * core - 4

    mine, far, near = (
        [ref[j, pl.ds(pl.multiple_of(core * 32, 32), 96), :] for j in range(2)]
        for ref in (mid_ref, far_ref, near_ref)
    )
    up = [jnp.where(core == 0, a, b) for a, b in zip(far, near)]
    down = [jnp.where(core == 0, b, a) for a, b in zip(far, near)]
    lat = jnp.concatenate(up + mine + down, axis=1)
    col = lax.broadcasted_iota(jnp.int32, (1, 512), 1) % 64
    for down in range(3):
        for side in range(3):
            offset = 64 * (1 + down) + side - 1
            piece = pltpu.roll(lat, 768 - offset, 1)[:, :512]
            if side == 0:
                piece = jnp.where(col == 0, 0.0, piece)
            if side == 2:
                piece = jnp.where(col == 63, 0.0, piece)
            hi, lo = split(piece)
            for f in range(6):
                at = f * 144 + (down * 3 + side) * 16
                taps_hi[at : at + 16, :] = hi[f * 16 : f * 16 + 16]
                taps_lo[at : at + 16, :] = lo[f * 16 : f * 16 + 16]

    def fill(p, part):
        for unit in range(9 * part, 9 * part + 9):
            side, rows = unit // 12, slice(unit % 12 * 32, unit % 12 * 32 + 32)
            lanes = slice(side * 384, side * 384 + 384)
            lags = []
            for down in range(3):
                if p < 2:
                    lags.append(raw[2 * p, down, side, rows, :])
                else:
                    even = raw[0, down, side, rows, :] + raw[2, down, side, rows, :]
                    odd = raw[1, down, side, rows, :]
                    lags.append(even + odd if p == 2 else even - odd)
            even = lags[0] + lags[2]
            for q, w in enumerate((lags[0], lags[2], even + lags[1], even - lags[1])):
                hi, lo = split(w)
                weights[p % 2, q, rows, lanes] = hi
                weights[p % 2, q, slice(rows.start + 384, rows.stop + 384), lanes] = lo

    b_in, gain, shift, b_mid = (ref[...][None] for ref in (b_in_ref, gain_ref, shift_ref, b_mid_ref))
    win_hi, win_lo = split(w_in_ref[...])
    row = lax.broadcasted_iota(jnp.int32, (512, 1), 0) // 64 + (4 * h - 2)
    row_ok = jnp.logical_and(row >= 0, row < 32)
    hidden = []
    for f in range(4):
        x_hi = taps_hi[f * 144 : f * 144 + 432, :]
        x_lo = taps_lo[f * 144 : f * 144 + 432, :]
        init = dot_rows(x_hi, win_hi) + dot_rows(x_lo, win_hi) + dot_rows(x_hi, win_lo)
        init = init + b_in
        if f >= 2:
            start[f - 2] = init[64:448]
        mean_square = jnp.mean(init * init, axis=-1, keepdims=True)
        value = init / jnp.sqrt(mean_square + EPS) * gain + shift
        value = value / (1.0 + jnp.exp(-value))
        hidden.append(jnp.where(jnp.logical_and(row_ok, first + f >= 0), value, 0.0))
        fill(0, f)

    d0, d1, d2, d3 = hidden
    for p, value in enumerate((d0 - d2, d1 - d3, 0.5 * (d1 + d2), 0.5 * (d2 - d1))):
        for i in range(3):
            r0, r1, r2, r3 = (value[(2 * i + n) * 64 : (2 * i + n) * 64 + 64] for n in range(4))
            rows = slice(i * 64, i * 64 + 64)
            for q, part in enumerate((r0 - r2, r1 - r3, 0.5 * (r1 + r2), 0.5 * (r2 - r1))):
                hi, lo = split(part)
                inner[p, q, rows, 0:384] = hi
                inner[p, q, rows, 384:768] = lo

    signs = (((0, 1),), ((1, -1),), ((0, 1), (1, 1)), ((0, 1), (1, -1)))
    filled = set()
    for p in range(4):
        for q in range(4):
            hi, lo = inner[p, q, :, 0:384], inner[p, q, :, 384:768]
            y = dot(jnp.concatenate([hi, hi], axis=1), weights[p % 2, q])
            y = y + dot(lo, weights[p % 2, q, 0:384, :])
            for j, frame_sign in signs[p]:
                for a, row_sign in signs[q]:
                    term = y if frame_sign * row_sign > 0 else -y
                    acc[j, a] = acc[j, a] + term if (j, a) in filled else term
                    filled.add((j, a))
            if p < 3:
                fill(p + 1, q)

    place = lax.broadcasted_iota(jnp.int32, (64, 1), 0)
    for j in range(2):
        for r in range(6):
            rows = slice((r // 2) * 64, (r // 2) * 64 + 64)
            left = jnp.where(place == 0, 0.0, pltpu.roll(acc[j, r % 2, rows, 0:384], 1, 0))
            right = jnp.where(place == 63, 0.0, pltpu.roll(acc[j, r % 2, rows, 768:1152], 63, 0))
            out = start[j, r * 64 : r * 64 + 64] + b_mid + left + acc[j, r % 2, rows, 384:768] + right
            own_ref[j, r * 64 : r * 64 + 64] = jnp.where(first + 2 + j >= 0, out, 0.0)
    send_ref[...] = own_ref[1 - core]


def upsample_kernel(
    own_ref, got_ref, w_time_ref, b_time_ref, w_up_ref, b_up_ref,
    out_ref,
    hist_hi, hist_lo, x_hi, x_lo, d_hi, d_lo, mixed,
):
    h, s = lax.axis_index("height"), lax.axis_index("seq")
    even_core = lax.rem(s, 2) == 0
    own0, own1, got = own_ref[0], own_ref[1], got_ref[...]
    frames = (
        jnp.where(even_core, own0, got),
        jnp.where(even_core, own1, own0),
        jnp.where(even_core, got, own1),
    )
    for lag, value in enumerate(frames):
        hist_hi[:, lag * 384 : lag * 384 + 384], hist_lo[:, lag * 384 : lag * 384 + 384] = split(value)
    t_hi, t_lo = split(w_time_ref[...])
    paired = dot(hist_hi[...], t_hi) + dot(hist_lo[...], t_hi) + dot(hist_hi[...], t_lo)
    row = lax.broadcasted_iota(jnp.int32, (384, 1), 0) // 64 + (4 * h - 1)
    paired = jnp.where(jnp.logical_and(row >= 0, row < 32), paired + b_time_ref[...][None], 0.0)

    place = lax.broadcasted_iota(jnp.int32, (384, 1), 0) % 64
    for f in range(2):
        x = paired[:, f * 384 : f * 384 + 384]
        left = jnp.where(place == 0, 0.0, pltpu.roll(x, 1, 0))
        right = jnp.where(place == 63, 0.0, pltpu.roll(x, 383, 0))
        for c, value in enumerate((left, x, right)):
            lanes = slice(c * 384, c * 384 + 384)
            x_hi[f, :, lanes], x_lo[f, :, lanes] = split(value[64:320])
            d_hi[f, :, lanes], d_lo[f, :, lanes] = split(value[0:320] - value[64:384])

    b_up = jnp.concatenate([b_up_ref[...][None], jnp.zeros((1, 64), F32)], axis=1)
    for b in range(2):
        weights = []
        for sel in ((0,), (0, 1, 2), (2,)):
            cols = [sum(w_up_ref[r, c] for r in sel) for c in range(3)]
            parts = (cols[0], cols[1] + cols[2]) if b == 0 else (cols[0] + cols[1], cols[2])
            both = jnp.concatenate(parts, axis=1)
            weights.append(split(jnp.concatenate([both, jnp.zeros((64, 768), F32)], axis=0)))
        lanes = slice(b * 384, b * 384 + 768)
        for f in range(2):
            def product(hi, lo, w):
                return dot_lanes(hi, w[0]) + dot_lanes(lo, w[0]) + dot_lanes(hi, w[1])

            m1 = product(d_hi[f, 0:256, lanes], d_lo[f, 0:256, lanes], weights[0])
            m2 = product(x_hi[f, :, lanes], x_lo[f, :, lanes], weights[1]) + b_up
            m3 = product(d_hi[f, 64:320, lanes], d_lo[f, 64:320, lanes], weights[2])
            for a, value in enumerate((m1 + m2, m2 - m3)):
                for i in range(4):
                    for j in range(2):
                        mixed[f, 2 * i + a, j, pl.ds(b, 64, stride=2), :] = value[
                            i * 64 : i * 64 + 64, j * 128 : j * 128 + 128
                        ]
    for f in range(2):
        for p in range(8):
            out_ref[f, p, 0:128, :] = mixed[f, p, 0].T
            out_ref[f, p, 128:192, :] = mixed[f, p, 1].T[0:64]


def pair_kernel(row_ref, other_ref, pair_ref):
    even_core = lax.rem(lax.axis_index("seq"), 2) == 0
    row, other = row_ref[...], other_ref[...]
    pair_ref[...] = jnp.concatenate(
        [jnp.where(even_core, row, other), jnp.where(even_core, other, row)], axis=1
    )


def frames_kernel(slab_ref, before_ref, beside_ref, frames_ref):
    s = lax.axis_index("seq")
    late, even_core = lax.div(s, 2) == 1, lax.rem(s, 2) == 0
    for j in range(2):
        before, beside, slab = before_ref[j], beside_ref[j], slab_ref[j]
        older = jnp.where(even_core, before, beside)[32:64]
        newer = jnp.where(even_core, beside, before)
        frames_ref[j, 0:32] = jnp.where(late, before[0:32], older)
        frames_ref[j, 32:64] = jnp.where(late, before[32:64], newer[0:32])
        frames_ref[j, 64:96] = jnp.where(late, slab[0:32], newer[32:64])
        frames_ref[j, 96:128] = jnp.where(late, slab[32:64], slab[0:32])


def assemble(kernel, shape, *parts):
    return pl.pallas_call(
        kernel,
        out_shape=jax.ShapeDtypeStruct(shape, F32),
        in_specs=[VMEM] * len(parts),
        out_specs=VMEM,
        cost_estimate=pl.CostEstimate(flops=COST, bytes_accessed=1 << 18, transcendentals=0),
        compiler_params=pltpu.CompilerParams(vmem_limit_bytes=2 << 20),
        name="assemble",
    )(*parts)


def gather_latents(latents):
    half = lax.axis_index("seq") // 2
    row = latents[0, :, :, 0, :].reshape(64, 64)
    other = send(row, lambda t, h, s: (t, h, s ^ 1))
    pair = assemble(pair_kernel, (64, 128), row, other)
    other = send(pair, lambda t, h, s: (t, h, s ^ 2))
    slab = jnp.where(half == 0, jnp.stack([pair, other]), jnp.stack([other, pair]))
    before = send(slab, lambda t, h, s: (t + 2 if s == 0 else t + 1, h, s))
    beside = send(before, lambda t, h, s: (t, h, s ^ 1) if s < 2 else None)
    frames = assemble(frames_kernel, (2, 128, 128), slab, before, beside)
    far = send(frames, lambda t, h, s: (t, h + 1 if s % 2 == 0 else h - 1, s))
    near = send(far, lambda t, h, s: (t, h, s ^ 1))
    return frames, far, near


def body(latents, w_in, b_in, norm_gain, norm_shift, w_mid, b_mid, w_time, b_time, w_up, b_up):
    frames, far, near = gather_latents(latents)
    own, outgoing = pl.pallas_call(
        blend_kernel,
        out_shape=(
            jax.ShapeDtypeStruct((2, 384, 384), F32),
            jax.ShapeDtypeStruct((384, 384), F32),
        ),
        in_specs=[VMEM] * 9,
        out_specs=(VMEM, VMEM),
        scratch_shapes=[
            pltpu.VMEM((864, 512), BF16),
            pltpu.VMEM((864, 512), BF16),
            pltpu.VMEM((2, 384, 384), F32),
            pltpu.VMEM((4, 4, 192, 768), BF16),
            pltpu.VMEM((2, 4, 768, 1152), BF16),
            pltpu.VMEM((2, 2, 192, 1152), F32),
        ],
        cost_estimate=pl.CostEstimate(flops=1_000_000, bytes_accessed=1 << 18, transcendentals=0),
        compiler_params=pltpu.CompilerParams(vmem_limit_bytes=36 << 20),
        name="blend",
    )(
        frames, far, near, w_in.reshape(432, 384), b_in, norm_gain, norm_shift, b_mid, w_mid,
    )
    got = send(outgoing, lambda t, h, s: (t, h, s ^ 1))
    out = pl.pallas_call(
        upsample_kernel,
        out_shape=jax.ShapeDtypeStruct((2, 8, 192, 128), F32),
        in_specs=[VMEM] * 6,
        out_specs=VMEM,
        scratch_shapes=[
            pltpu.VMEM((384, 1152), BF16),
            pltpu.VMEM((384, 1152), BF16),
            pltpu.VMEM((2, 256, 1152), BF16),
            pltpu.VMEM((2, 256, 1152), BF16),
            pltpu.VMEM((2, 320, 1152), BF16),
            pltpu.VMEM((2, 320, 1152), BF16),
            pltpu.VMEM((2, 8, 2, 128, 128), F32),
        ],
        compiler_params=pltpu.CompilerParams(vmem_limit_bytes=26 << 20),
        name="upsample",
    )(own, got, w_time.reshape(1152, 768), b_time, jnp.swapaxes(w_up, 2, 3), b_up)
    return jnp.swapaxes(out, 2, 3)[None]


def solution(mesh):
    placed = (P(None, "tm", None, ("height", "seq"), None),) + (P(),) * 10
    return jax.shard_map(
        body,
        mesh=mesh,
        in_specs=placed,
        out_specs=P(None, ("tm", "seq"), "height", None, None),
        check_vma=False,
    )
```

time: 80.8 us -> 63.7 us (0.79)
  local copies, waits for them, and re-layouts: 12.8 us -> 0.82 us
  Pallas kernels: 38.3 us -> 31.4 us
  waiting for transfers between devices: 7.64 us -> 12.6 us
  other arithmetic: 1.85 us -> 0.01 us
  starting transfers between devices: 19.6 us -> 18.5 us
    broadcast_in_dim x6 -> x0, local copies, waits for them, and re-layouts: 8.4 us -> none  [the longest x1 2.78 us: body(): return out[None]]
    ppermute x7, waiting for transfers between devices: 7.64 us -> 12.6 us  [send(): return lax.ppermute(value, AXES, pairs)]
    pallas_call x1, Pallas kernels: 25.7 us -> 22 us  [body(): pl.pallas_call(blend_kernel, out_shape=(jax.ShapeDtypeStruct((2, 384, 384...]
    unnamed x13 -> x22, local copies, waits for them, and re-layouts: 4.39 us -> 0.82 us
    pallas_call x1 -> x3, Pallas kernels: 12.6 us -> 9.33 us  [the longest x1 9.23 us: body(): pl.pallas_call(upsample_kernel, out_shape=jax.ShapeDtypeStruct((2, 8, 192...]
    select_n x3 -> x0, other arithmetic: 1.85 us -> none  [the longest x2 1.83 us: gather_latents(): jnp.where(core == 0, jnp.concatenate([row, other], axis=-1), jnp.concaten...]
    ppermute x7, starting transfers between devices: 19.6 us -> 18.5 us  [send(): return lax.ppermute(value, AXES, pairs)]
  transfers between devices with their start and end apart: 7 -> 7, of which waited for: 5 -> 7; matrix products, arithmetic and copies ran while one was open for 12% -> 0% of each run, Pallas kernels for 0% -> 0%
where the time goes in v1:
time: 63.7 us; the launch traced here: 63.5 us
  Pallas kernels  31.4 us (49%)
  starting transfers between devices  18.5 us (29%)
  waiting for transfers between devices  12.6 us (20%)
  local copies, waits for them, and re-layouts  0.82 us (1%)
    pallas_call x1, Pallas kernels, body(): pl.pallas_call(blend_kernel, out_shape=(jax.ShapeDtypeStruct((2, 384, 384...  22 us
    ppermute x7, starting transfers between devices, send(): return lax.ppermute(value, AXES, pairs)  18.5 us
    ppermute x7, waiting for transfers between devices, send(): return lax.ppermute(value, AXES, pairs)  12.6 us
    pallas_call x1, Pallas kernels, body(): pl.pallas_call(upsample_kernel, out_shape=jax.ShapeDtypeStruct((2, 8, 192...  9.23 us
  transfers between devices with their start and end apart: 7, of which 7 were waited for; matrix products, arithmetic and copies ran while one was open for 0% of the time, Pallas kernels for 0%

profile of v1, /device:TPU:27, one launch (start us, length us, event | category | flops | bytes accessed | tf_op | source)
XLA Modules:
  0.0 63.5 jit_solution(13687626993836451339)
XLA Ops:
  0.0 0.7 %collective-permute-start = (f32[64,64]{1,0:T(8,128)}, f32[64,64]{1,0:T(8,128)S(1)}, u32[]{:S(2)}, u32[]{:S(2)}) collective-permute-start(f32[64,64]{1,0:T(8,128)} %bitcast.13), channel_id=1, source_target_pairs={{0,1},{1,0},{2,3},{3,2},{4,5},{5,4},{6,7},{7,6},{8,9},{9,8},{10,11... | collective-permute-start | bytes 49160 | tf_op jit(solution)/shard_map/ppermute | solution.py:43
  0.7 1.1 %collective-permute-done.other_ref = f32[64,64]{1,0:T(8,128)S(1)} collective-permute-done((f32[64,64]{1,0:T(8,128)}, f32[64,64]{1,0:T(8,128)S(1)}, u32[]{:S(2)}, u32[]{:S(2)}) %collective-permute-start) | collective-permute-done | bytes 16416 | tf_op jit(solution)/shard_map/ppermute | solution.py:43
  1.7 0.0 copy-start.10
  1.7 0.8 %copy-done.10 = f32[1,4,16,1,64]{4,3,2,1,0:T(1,128)S(1)} copy-done((f32[1,4,16,1,64]{4,3,2,1,0:T(1,128)S(1)}, f32[1,4,16,1,64]{4,3,2,1,0:T(1,128)}, u32[]{:S(2)}) %copy-start.10) | copy-done | bytes 16408
  2.5 0.1 assemble.2
  2.6 1.9 %collective-permute-start.1 = (f32[64,128]{1,0:T(8,128)S(1)}, f32[64,128]{1,0:T(8,128)S(1)}, u32[]{:S(2)}, u32[]{:S(2)}) collective-permute-start(f32[64,128]{1,0:T(8,128)S(1)} %assemble.2), channel_id=1, source_target_pairs={{0,2},{1,3},{2,0},{3,1},{4,6},{5,7},{6,4},{7,5},{8,10},{9,11},{10,... | collective-permute-start | bytes 98312 | tf_op jit(solution)/shard_map/ppermute | solution.py:43
  4.4 2.4 %collective-permute-done.1 = f32[64,128]{1,0:T(8,128)S(1)} collective-permute-done((f32[64,128]{1,0:T(8,128)S(1)}, f32[64,128]{1,0:T(8,128)S(1)}, u32[]{:S(2)}, u32[]{:S(2)}) %collective-permute-start.1) | collective-permute-done | bytes 32800 | tf_op jit(solution)/shard_map/ppermute | solution.py:43
  6.9 0.0 copy-start.3
  6.9 0.0 copy-start.5
  6.9 0.0 copy-start.6
  6.9 0.0 copy-start.7
  6.9 0.0 copy-start.8
  6.9 1.4 %collective-permute-start.2 = (f32[2,64,128]{2,1,0:T(8,128)S(1)}, f32[2,64,128]{2,1,0:T(8,128)S(1)}, u32[]{:S(2)}, u32[]{:S(2)}) collective-permute-start(f32[2,64,128]{2,1,0:T(8,128)S(1)} %maximum_select_fusion.slab_ref), channel_id=1, source_target_pairs={{0,64},{1,33},{2,34},{3,35},{4,68},{5,37},{6,38},{7,39},{8,72},{9,... | collective-permute-start | bytes 196616 | tf_op jit(solution)/shard_map/ppermute | solution.py:43
  8.4 3.7 %collective-permute-done.2.before_ref = f32[2,64,128]{2,1,0:T(8,128)S(1)} collective-permute-done((f32[2,64,128]{2,1,0:T(8,128)S(1)}, f32[2,64,128]{2,1,0:T(8,128)S(1)}, u32[]{:S(2)}, u32[]{:S(2)}) %collective-permute-start.2) | collective-permute-done | bytes 65568 | tf_op jit(solution)/shard_map/ppermute | solution.py:43
  12.1 6.0 %collective-permute-start.3 = (f32[2,64,128]{2,1,0:T(8,128)S(1)}, f32[2,64,128]{2,1,0:T(8,128)S(1)}, u32[]{:S(2)}, u32[]{:S(2)}) collective-permute-start(f32[2,64,128]{2,1,0:T(8,128)S(1)} %collective-permute-done.2.before_ref), channel_id=1, source_target_pairs={{0,1},{1,0},{4,5},{5,4},{8,9},{9,8},{12,13},{13,12},{16,17},{17,16... | collective-permute-start | bytes 196616 | tf_op jit(solution)/shard_map/ppermute | solution.py:43
  18.1 0.9 %collective-permute-done.3.beside_ref = f32[2,64,128]{2,1,0:T(8,128)S(1)} collective-permute-done((f32[2,64,128]{2,1,0:T(8,128)S(1)}, f32[2,64,128]{2,1,0:T(8,128)S(1)}, u32[]{:S(2)}, u32[]{:S(2)}) %collective-permute-start.3) | collective-permute-done | bytes 65568 | tf_op jit(solution)/shard_map/ppermute | solution.py:43
  19.0 0.0 copy-start
  19.1 5.9 %collective-permute-start.4 = (f32[2,128,128]{2,1,0:T(8,128)S(1)}, f32[2,128,128]{2,1,0:T(8,128)S(1)}, u32[]{:S(2)}, u32[]{:S(2)}) collective-permute-start(f32[2,128,128]{2,1,0:T(8,128)S(1)} %assemble.3.mid_ref), channel_id=1, source_target_pairs={{0,4},{2,6},{4,8},{5,1},{6,10},{7,3},{8,12},{9,5},{10,14},{11,7},{... | collective-permute-start | bytes 393224 | tf_op jit(solution)/shard_map/ppermute | solution.py:43
  25.0 1.9 %collective-permute-done.4.far_ref = f32[2,128,128]{2,1,0:T(8,128)S(1)} collective-permute-done((f32[2,128,128]{2,1,0:T(8,128)S(1)}, f32[2,128,128]{2,1,0:T(8,128)S(1)}, u32[]{:S(2)}, u32[]{:S(2)}) %collective-permute-start.4) | collective-permute-done | bytes 131104 | tf_op jit(solution)/shard_map/ppermute | solution.py:43
  26.9 1.9 %collective-permute-start.5 = (f32[2,128,128]{2,1,0:T(8,128)S(1)}, f32[2,128,128]{2,1,0:T(8,128)S(1)}, u32[]{:S(2)}, u32[]{:S(2)}) collective-permute-start(f32[2,128,128]{2,1,0:T(8,128)S(1)} %collective-permute-done.4.far_ref), channel_id=1, source_target_pairs={{0,1},{1,0},{2,3},{3,2},{4,5},{5,4},{6,7},{7,6},{8,9},{9,8},{10,11... | collective-permute-start | bytes 393224 | tf_op jit(solution)/shard_map/ppermute | solution.py:43
  28.8 1.0 %collective-permute-done.5.near_ref = f32[2,128,128]{2,1,0:T(8,128)S(1)} collective-permute-done((f32[2,128,128]{2,1,0:T(8,128)S(1)}, f32[2,128,128]{2,1,0:T(8,128)S(1)}, u32[]{:S(2)}, u32[]{:S(2)}) %collective-permute-start.5) | collective-permute-done | bytes 131104 | tf_op jit(solution)/shard_map/ppermute | solution.py:43
  29.8 0.0 copy-done.3
  29.8 0.0 copy-done.5
  29.8 0.0 copy-done.6
  29.8 0.0 copy-done.7
  29.8 0.0 copy-done.8
  29.8 0.0 copy-done
  29.8 0.0 copy-start.1
  29.8 0.0 copy-start.2
  29.8 0.0 copy-start.4
  29.8 0.0 copy-start.9
  29.8 22.0 %blend.1 = (f32[2,384,384]{2,1,0:T(8,128)S(1)}, f32[384,384]{1,0:T(8,128)S(1)}) custom-call(f32[2,128,128]{2,1,0:T(8,128)S(1)} %assemble.3.mid_ref, f32[2,128,128]{2,1,0:T(8,128)S(1)} %collective-permute-done.4.far_ref, f32[2,128,128]{2,1,0:T(8,128)S(1)} %collective-permute-done.5.near_ref, f32[432,384]{1,0:T(8,128)S(1)} %bitcast.11, f32[384]{0:T(512)S(1)} %copy-done.5, ...), custom_call_target="tpu_custom_call" | custom-call | flops 1000000 | bytes 262144 | tf_op jit(solution)/shard_map/blend/pallas_call | solution.py:257
  51.9 0.7 %collective-permute-start.6 = (f32[384,384]{1,0:T(8,128)S(1)}, f32[384,384]{1,0:T(8,128)S(1)}, u32[]{:S(2)}, u32[]{:S(2)}) collective-permute-start(f32[384,384]{1,0:T(8,128)S(1)} %get-tuple-element.8), channel_id=1, source_target_pairs={{0,1},{1,0},{2,3},{3,2},{4,5},{5,4},{6,7},{7,6},{8,9},{9,8},{10,11... | collective-permute-start | bytes 1769480 | tf_op jit(solution)/shard_map/ppermute | solution.py:43
  52.6 1.6 %collective-permute-done.6.got_ref = f32[384,384]{1,0:T(8,128)S(1)} collective-permute-done((f32[384,384]{1,0:T(8,128)S(1)}, f32[384,384]{1,0:T(8,128)S(1)}, u32[]{:S(2)}, u32[]{:S(2)}) %collective-permute-start.6) | collective-permute-done | bytes 589856 | tf_op jit(solution)/shard_map/ppermute | solution.py:43
  54.2 0.0 copy-done.1
  54.2 0.0 copy-done.2
  54.2 0.0 copy-done.4
  54.2 0.0 copy-done.9
  54.2 9.2 %upsample.1 = f32[2,8,192,128]{3,2,1,0:T(8,128)} custom-call(f32[2,384,384]{2,1,0:T(8,128)S(1)} %get-tuple-element.7.own_ref, f32[384,384]{1,0:T(8,128)S(1)} %collective-permute-done.6.got_ref, f32[1152,768]{1,0:T(8,128)S(1)} %bitcast.9, f32[768]{0:T(1024)S(1)} %copy-done.4, f32[3,3,192,384]{3,2,1,0:T(8,128)S(1)} %bitcast.10, f32[192]{0:T(256)S(1)} %copy-done.9), custom_call_target="tpu_custom_call" | custom-call | tf_op jit(solution)/shard_map/upsample/pallas_call | solution.py:280
  (2 shorter events, 0.0 us)
Async XLA Ops:
  0.0 1.7 %collective-permute-start = (f32[64,64]{1,0:T(8,128)}, f32[64,64]{1,0:T(8,128)S(1)}, u32[]{:S(2)}, u32[]{:S(2)}) collective-permute-start(f32[64,64]{1,0:T(8,128)} %bitcast.13), channel_id=1, source_target_pairs={{0,1},{1,0},{2,3},{3,2},{4,5},{5,4},{6,7},{7,6},{8,9},{9,8},{10,11... | collective-permute-start | bytes 49160 | tf_op jit(solution)/shard_map/ppermute | solution.py:43
  1.7 0.8 %copy-start.10 = (f32[1,4,16,1,64]{4,3,2,1,0:T(1,128)S(1)}, f32[1,4,16,1,64]{4,3,2,1,0:T(1,128)}, u32[]{:S(2)}) copy-start(f32[1,4,16,1,64]{4,3,2,1,0:T(1,128)} %param.11) | copy-start | bytes 49156
  2.6 4.3 %collective-permute-start.1 = (f32[64,128]{1,0:T(8,128)S(1)}, f32[64,128]{1,0:T(8,128)S(1)}, u32[]{:S(2)}, u32[]{:S(2)}) collective-permute-start(f32[64,128]{1,0:T(8,128)S(1)} %assemble.2), channel_id=1, source_target_pairs={{0,2},{1,3},{2,0},{3,1},{4,6},{5,7},{6,4},{7,5},{8,10},{9,11},{10,... | collective-permute-start | bytes 98312 | tf_op jit(solution)/shard_map/ppermute | solution.py:43
  6.9 22.9 %copy-start.3 = (f32[3,3,3,16,384]{4,3,2,1,0:T(8,128)S(1)}, f32[3,3,3,16,384]{4,3,2,1,0:T(8,128)}, u32[]{:S(2)}) copy-start(f32[3,3,3,16,384]{4,3,2,1,0:T(8,128)} %param.12) | copy-start | bytes 1990660
  6.9 22.9 %copy-start.5 = (f32[384]{0:T(512)S(1)}, f32[384]{0:T(512)}, u32[]{:S(2)}) copy-start(f32[384]{0:T(512)} %b_in_ref.1) | copy-start | bytes 4612
  6.9 22.9 %copy-start.6 = (f32[384]{0:T(512)S(1)}, f32[384]{0:T(512)}, u32[]{:S(2)}) copy-start(f32[384]{0:T(512)} %gain_ref.1) | copy-start | bytes 4612
  6.9 22.8 %copy-start.7 = (f32[384]{0:T(512)S(1)}, f32[384]{0:T(512)}, u32[]{:S(2)}) copy-start(f32[384]{0:T(512)} %shift_ref.1) | copy-start | bytes 4612
  6.9 22.8 %copy-start.8 = (f32[384]{0:T(512)S(1)}, f32[384]{0:T(512)}, u32[]{:S(2)}) copy-start(f32[384]{0:T(512)} %b_mid_ref.1) | copy-start | bytes 4612
  6.9 5.1 %collective-permute-start.2 = (f32[2,64,128]{2,1,0:T(8,128)S(1)}, f32[2,64,128]{2,1,0:T(8,128)S(1)}, u32[]{:S(2)}, u32[]{:S(2)}) collective-permute-start(f32[2,64,128]{2,1,0:T(8,128)S(1)} %maximum_select_fusion.slab_ref), channel_id=1, source_target_pairs={{0,64},{1,33},{2,34},{3,35},{4,68},{5,37},{6,38},{7,39},{8,72},{9,... | collective-permute-start | bytes 196616 | tf_op jit(solution)/shard_map/ppermute | solution.py:43
  12.1 6.9 %collective-permute-start.3 = (f32[2,64,128]{2,1,0:T(8,128)S(1)}, f32[2,64,128]{2,1,0:T(8,128)S(1)}, u32[]{:S(2)}, u32[]{:S(2)}) collective-permute-start(f32[2,64,128]{2,1,0:T(8,128)S(1)} %collective-permute-done.2.before_ref), channel_id=1, source_target_pairs={{0,1},{1,0},{4,5},{5,4},{8,9},{9,8},{12,13},{13,12},{16,17},{17,16... | collective-permute-start | bytes 196616 | tf_op jit(solution)/shard_map/ppermute | solution.py:43
  19.0 10.8 %copy-start = (f32[3,3,3,384,384]{4,3,2,1,0:T(8,128)S(1)}, f32[3,3,3,384,384]{4,3,2,1,0:T(8,128)}, u32[]{:S(2)}) copy-start(f32[3,3,3,384,384]{4,3,2,1,0:T(8,128)} %raw.1) | copy-start | bytes 47775748
  19.1 7.8 %collective-permute-start.4 = (f32[2,128,128]{2,1,0:T(8,128)S(1)}, f32[2,128,128]{2,1,0:T(8,128)S(1)}, u32[]{:S(2)}, u32[]{:S(2)}) collective-permute-start(f32[2,128,128]{2,1,0:T(8,128)S(1)} %assemble.3.mid_ref), channel_id=1, source_target_pairs={{0,4},{2,6},{4,8},{5,1},{6,10},{7,3},{8,12},{9,5},{10,14},{11,7},{... | collective-permute-start | bytes 393224 | tf_op jit(solution)/shard_map/ppermute | solution.py:43
  26.9 2.9 %collective-permute-start.5 = (f32[2,128,128]{2,1,0:T(8,128)S(1)}, f32[2,128,128]{2,1,0:T(8,128)S(1)}, u32[]{:S(2)}, u32[]{:S(2)}) collective-permute-start(f32[2,128,128]{2,1,0:T(8,128)S(1)} %collective-permute-done.4.far_ref), channel_id=1, source_target_pairs={{0,1},{1,0},{2,3},{3,2},{4,5},{5,4},{6,7},{7,6},{8,9},{9,8},{10,11... | collective-permute-start | bytes 393224 | tf_op jit(solution)/shard_map/ppermute | solution.py:43
  29.8 24.4 %copy-start.1 = (f32[3,384,768]{2,1,0:T(8,128)S(1)}, f32[3,384,768]{2,1,0:T(8,128)}, u32[]{:S(2)}) copy-start(f32[3,384,768]{2,1,0:T(8,128)} %param.18) | copy-start | bytes 10616836
  29.8 24.4 %copy-start.2 = (f32[3,3,384,192]{2,3,1,0:T(8,128)S(1)}, f32[3,3,384,192]{2,3,1,0:T(8,128)}, u32[]{:S(2)}) copy-start(f32[3,3,384,192]{2,3,1,0:T(8,128)} %param.20) | copy-start | bytes 7962628
  29.8 24.4 %copy-start.4 = (f32[768]{0:T(1024)S(1)}, f32[768]{0:T(1024)}, u32[]{:S(2)}) copy-start(f32[768]{0:T(1024)} %b_time_ref.1) | copy-start | bytes 9220
  29.8 24.4 %copy-start.9 = (f32[192]{0:T(256)S(1)}, f32[192]{0:T(256)}, u32[]{:S(2)}) copy-start(f32[192]{0:T(256)} %b_up_ref.1) | copy-start | bytes 2308
  51.9 2.3 %collective-permute-start.6 = (f32[384,384]{1,0:T(8,128)S(1)}, f32[384,384]{1,0:T(8,128)S(1)}, u32[]{:S(2)}, u32[]{:S(2)}) collective-permute-start(f32[384,384]{1,0:T(8,128)S(1)} %get-tuple-element.8), channel_id=1, source_target_pairs={{0,1},{1,0},{2,3},{3,2},{4,5},{5,4},{6,7},{7,6},{8,9},{9,8},{10,11... | collective-permute-start | bytes 1769480 | tf_op jit(solution)/shard_map/ppermute | solution.py:43

commit v2 on v1

--- a/solution.py
+++ b/solution.py
@@ -43,10 +43,39 @@
     return lax.ppermute(value, AXES, pairs)
 
 
+def weights_kernel(raw, weights):
+    def rows_of(n, carry):
+        hi_rows = pl.ds(pl.multiple_of(n * 16, 16), 16)
+        lo_rows = pl.ds(pl.multiple_of(n * 16 + 384, 16), 16)
+        for side in range(3):
+            for channel in range(0, 384, 128):
+                taps = [
+                    [raw[lag, down, side, hi_rows, channel : channel + 128] for down in range(3)]
+                    for lag in range(3)
+                ]
+                even = [taps[0][down] + taps[2][down] for down in range(3)]
+                over_frames = (
+                    taps[0],
+                    taps[2],
+                    [even[down] + taps[1][down] for down in range(3)],
+                    [even[down] - taps[1][down] for down in range(3)],
+                )
+                lanes = slice(side * 384 + channel, side * 384 + channel + 128)
+                for p, (above, at, below) in enumerate(over_frames):
+                    outer = above + below
+                    for q, w in enumerate((above, below, outer + at, outer - at)):
+                        hi, lo = split(w)
+                        weights[p, q, hi_rows, lanes] = hi
+                        weights[p, q, lo_rows, lanes] = lo
+        return carry
+
+    lax.fori_loop(0, 24, rows_of, 0)
+
+
 def blend_kernel(
-    mid_ref, far_ref, near_ref, w_in_ref, b_in_ref, gain_ref, shift_ref, b_mid_ref, raw,
+    mid_ref, far_ref, near_ref, w_in_ref, b_in_ref, gain_ref, shift_ref, b_mid_ref, weights,
     own_ref, send_ref,
-    taps_hi, taps_lo, start, inner, weights, acc,
+    taps_hi, taps_lo, start, inner, acc,
 ):
     t, h, s = (lax.axis_index(axis) for axis in AXES)
     core = lax.rem(s, 2)
@@ -74,24 +103,6 @@
                 taps_hi[at : at + 16, :] = hi[f * 16 : f * 16 + 16]
                 taps_lo[at : at + 16, :] = lo[f * 16 : f * 16 + 16]
 
-    def fill(p, part):
-        for unit in range(9 * part, 9 * part + 9):
-            side, rows = unit // 12, slice(unit % 12 * 32, unit % 12 * 32 + 32)
-            lanes = slice(side * 384, side * 384 + 384)
-            lags = []
-            for down in range(3):
-                if p < 2:
-                    lags.append(raw[2 * p, down, side, rows, :])
-                else:
-                    even = raw[0, down, side, rows, :] + raw[2, down, side, rows, :]
-                    odd = raw[1, down, side, rows, :]
-                    lags.append(even + odd if p == 2 else even - odd)
-            even = lags[0] + lags[2]
-            for q, w in enumerate((lags[0], lags[2], even + lags[1], even - lags[1])):
-                hi, lo = split(w)
-                weights[p % 2, q, rows, lanes] = hi
-                weights[p % 2, q, slice(rows.start + 384, rows.stop + 384), lanes] = lo
-
     b_in, gain, shift, b_mid = (ref[...][None] for ref in (b_in_ref, gain_ref, shift_ref, b_mid_ref))
     win_hi, win_lo = split(w_in_ref[...])
     row = lax.broadcasted_iota(jnp.int32, (512, 1), 0) // 64 + (4 * h - 2)
@@ -108,7 +119,6 @@
         value = init / jnp.sqrt(mean_square + EPS) * gain + shift
         value = value / (1.0 + jnp.exp(-value))
         hidden.append(jnp.where(jnp.logical_and(row_ok, first + f >= 0), value, 0.0))
-        fill(0, f)
 
     d0, d1, d2, d3 = hidden
     for p, value in enumerate((d0 - d2, d1 - d3, 0.5 * (d1 + d2), 0.5 * (d2 - d1))):
@@ -125,15 +135,13 @@
     for p in range(4):
         for q in range(4):
             hi, lo = inner[p, q, :, 0:384], inner[p, q, :, 384:768]
-            y = dot(jnp.concatenate([hi, hi], axis=1), weights[p % 2, q])
-            y = y + dot(lo, weights[p % 2, q, 0:384, :])
+            y = dot(jnp.concatenate([hi, hi], axis=1), weights[p, q])
+            y = y + dot(lo, weights[p, q, 0:384, :])
             for j, frame_sign in signs[p]:
                 for a, row_sign in signs[q]:
                     term = y if frame_sign * row_sign > 0 else -y
                     acc[j, a] = acc[j, a] + term if (j, a) in filled else term
                     filled.add((j, a))
-            if p < 3:
-                fill(p + 1, q)
 
     place = lax.broadcasted_iota(jnp.int32, (64, 1), 0)
     for j in range(2):
@@ -254,6 +262,15 @@
 
 def body(latents, w_in, b_in, norm_gain, norm_shift, w_mid, b_mid, w_time, b_time, w_up, b_up):
     frames, far, near = gather_latents(latents)
+    weights = pl.pallas_call(
+        weights_kernel,
+        out_shape=jax.ShapeDtypeStruct((4, 4, 768, 1152), BF16),
+        in_specs=[VMEM],
+        out_specs=VMEM,
+        cost_estimate=pl.CostEstimate(flops=4_000_000_000, bytes_accessed=1 << 18, transcendentals=0),
+        compiler_params=pltpu.CompilerParams(vmem_limit_bytes=1 << 20),
+        name="weights",
+    )(w_mid)
     own, outgoing = pl.pallas_call(
         blend_kernel,
         out_shape=(
@@ -267,14 +284,13 @@
             pltpu.VMEM((864, 512), BF16),
             pltpu.VMEM((2, 384, 384), F32),
             pltpu.VMEM((4, 4, 192, 768), BF16),
-            pltpu.VMEM((2, 4, 768, 1152), BF16),
             pltpu.VMEM((2, 2, 192, 1152), F32),
         ],
         cost_estimate=pl.CostEstimate(flops=1_000_000, bytes_accessed=1 << 18, transcendentals=0),
-        compiler_params=pltpu.CompilerParams(vmem_limit_bytes=36 << 20),
+        compiler_params=pltpu.CompilerParams(vmem_limit_bytes=24 << 20),
         name="blend",
     )(
-        frames, far, near, w_in.reshape(432, 384), b_in, norm_gain, norm_shift, b_mid, w_mid,
+        frames, far, near, w_in.reshape(432, 384), b_in, norm_gain, norm_shift, b_mid, weights,
     )
     got = send(outgoing, lambda t, h, s: (t, h, s ^ 1))
     out = pl.pallas_call(
@@ -291,7 +307,7 @@
             pltpu.VMEM((2, 320, 1152), BF16),
             pltpu.VMEM((2, 8, 2, 128, 128), F32),
         ],
-        compiler_params=pltpu.CompilerParams(vmem_limit_bytes=26 << 20),
+        compiler_params=pltpu.CompilerParams(vmem_limit_bytes=24 << 20),
         name="upsample",
     )(own, got, w_time.reshape(1152, 768), b_time, jnp.swapaxes(w_up, 2, 3), b_up)
     return jnp.swapaxes(out, 2, 3)[None]

time: 63.7 us -> 62.7 us (0.984)
  starting transfers between devices: 18.5 us -> 17.8 us
    pallas_call x0 -> x1, Pallas kernels: none -> 5.95 us  [body(): pl.pallas_call(weights_kernel, out_shape=jax.ShapeDtypeStruct((4, 4, 768,...]
    pallas_call x1, Pallas kernels: 22 us -> 16.5 us  [body(): pl.pallas_call(blend_kernel, out_shape=(jax.ShapeDtypeStruct((2, 384, 384...]
    ppermute x7, starting transfers between devices: 18.5 us -> 17.8 us  [send(): return lax.ppermute(value, AXES, pairs)]
  transfers between devices with their start and end apart: 7 -> 7, of which waited for: 7 -> 6; matrix products, arithmetic and copies ran while one was open for 0% -> 0% of each run, Pallas kernels for 0% -> 10%
where the time goes in v2:
time: 62.7 us; the launch traced here: 62.5 us
  Pallas kernels  31.7 us (51%)
  starting transfers between devices  17.8 us (28%)
  waiting for transfers between devices  12 us (19%)
  local copies, waits for them, and re-layouts  0.82 us (1%)
    ppermute x7, starting transfers between devices, send(): return lax.ppermute(value, AXES, pairs)  17.8 us
    pallas_call x1, Pallas kernels, body(): pl.pallas_call(blend_kernel, out_shape=(jax.ShapeDtypeStruct((2, 384, 384...  16.5 us
    ppermute x7, waiting for transfers between devices, send(): return lax.ppermute(value, AXES, pairs)  12 us
    pallas_call x1, Pallas kernels, body(): pl.pallas_call(upsample_kernel, out_shape=jax.ShapeDtypeStruct((2, 8, 192...  9.23 us
    pallas_call x1, Pallas kernels, body(): pl.pallas_call(weights_kernel, out_shape=jax.ShapeDtypeStruct((4, 4, 768,...  5.95 us
  transfers between devices with their start and end apart: 7, of which 6 were waited for; matrix products, arithmetic and copies ran while one was open for 0% of the time, Pallas kernels for 10%

profile of v2, /device:TPU:27, one launch (start us, length us, event | category | flops | bytes accessed | tf_op | source)
XLA Modules:
  0.0 62.5 jit_solution(1399904849373665661)
XLA Ops:
  0.0 0.7 %collective-permute-start = (f32[64,64]{1,0:T(8,128)}, f32[64,64]{1,0:T(8,128)S(1)}, u32[]{:S(2)}, u32[]{:S(2)}) collective-permute-start(f32[64,64]{1,0:T(8,128)} %bitcast.13), channel_id=1, source_target_pairs={{0,1},{1,0},{2,3},{3,2},{4,5},{5,4},{6,7},{7,6},{8,9},{9,8},{10,11... | collective-permute-start | bytes 49160 | tf_op jit(solution)/shard_map/ppermute | solution.py:43
  0.7 1.1 %collective-permute-done.other_ref = f32[64,64]{1,0:T(8,128)S(1)} collective-permute-done((f32[64,64]{1,0:T(8,128)}, f32[64,64]{1,0:T(8,128)S(1)}, u32[]{:S(2)}, u32[]{:S(2)}) %collective-permute-start) | collective-permute-done | bytes 16416 | tf_op jit(solution)/shard_map/ppermute | solution.py:43
  1.7 0.0 copy-start.10
  1.7 0.8 %copy-done.10 = f32[1,4,16,1,64]{4,3,2,1,0:T(1,128)S(1)} copy-done((f32[1,4,16,1,64]{4,3,2,1,0:T(1,128)S(1)}, f32[1,4,16,1,64]{4,3,2,1,0:T(1,128)}, u32[]{:S(2)}) %copy-start.10) | copy-done | bytes 16408
  2.5 0.1 assemble.2
  2.6 1.9 %collective-permute-start.1 = (f32[64,128]{1,0:T(8,128)S(1)}, f32[64,128]{1,0:T(8,128)S(1)}, u32[]{:S(2)}, u32[]{:S(2)}) collective-permute-start(f32[64,128]{1,0:T(8,128)S(1)} %assemble.2), channel_id=1, source_target_pairs={{0,2},{1,3},{2,0},{3,1},{4,6},{5,7},{6,4},{7,5},{8,10},{9,11},{10,... | collective-permute-start | bytes 98312 | tf_op jit(solution)/shard_map/ppermute | solution.py:43
  4.4 2.4 %collective-permute-done.1 = f32[64,128]{1,0:T(8,128)S(1)} collective-permute-done((f32[64,128]{1,0:T(8,128)S(1)}, f32[64,128]{1,0:T(8,128)S(1)}, u32[]{:S(2)}, u32[]{:S(2)}) %collective-permute-start.1) | collective-permute-done | bytes 32800 | tf_op jit(solution)/shard_map/ppermute | solution.py:43
  6.9 1.3 %collective-permute-start.2 = (f32[2,64,128]{2,1,0:T(8,128)S(1)}, f32[2,64,128]{2,1,0:T(8,128)S(1)}, u32[]{:S(2)}, u32[]{:S(2)}) collective-permute-start(f32[2,64,128]{2,1,0:T(8,128)S(1)} %maximum_select_fusion.slab_ref), channel_id=1, source_target_pairs={{0,64},{1,33},{2,34},{3,35},{4,68},{5,37},{6,38},{7,39},{8,72},{9,... | collective-permute-start | bytes 196616 | tf_op jit(solution)/shard_map/ppermute | solution.py:43
  8.2 3.7 %collective-permute-done.2.before_ref = f32[2,64,128]{2,1,0:T(8,128)S(1)} collective-permute-done((f32[2,64,128]{2,1,0:T(8,128)S(1)}, f32[2,64,128]{2,1,0:T(8,128)S(1)}, u32[]{:S(2)}, u32[]{:S(2)}) %collective-permute-start.2) | collective-permute-done | bytes 65568 | tf_op jit(solution)/shard_map/ppermute | solution.py:43
  11.9 6.0 %collective-permute-start.3 = (f32[2,64,128]{2,1,0:T(8,128)S(1)}, f32[2,64,128]{2,1,0:T(8,128)S(1)}, u32[]{:S(2)}, u32[]{:S(2)}) collective-permute-start(f32[2,64,128]{2,1,0:T(8,128)S(1)} %collective-permute-done.2.before_ref), channel_id=1, source_target_pairs={{0,1},{1,0},{4,5},{5,4},{8,9},{9,8},{12,13},{13,12},{16,17},{17,16... | collective-permute-start | bytes 196616 | tf_op jit(solution)/shard_map/ppermute | solution.py:43
  18.0 0.9 %collective-permute-done.3.beside_ref = f32[2,64,128]{2,1,0:T(8,128)S(1)} collective-permute-done((f32[2,64,128]{2,1,0:T(8,128)S(1)}, f32[2,64,128]{2,1,0:T(8,128)S(1)}, u32[]{:S(2)}, u32[]{:S(2)}) %collective-permute-start.3) | collective-permute-done | bytes 65568 | tf_op jit(solution)/shard_map/ppermute | solution.py:43
  18.8 0.0 copy-start
  18.9 0.0 copy-start.3
  18.9 0.0 copy-start.5
  18.9 0.0 copy-start.6
  18.9 0.0 copy-start.7
  18.9 0.0 copy-start.8
  18.9 5.9 %collective-permute-start.4 = (f32[2,128,128]{2,1,0:T(8,128)S(1)}, f32[2,128,128]{2,1,0:T(8,128)S(1)}, u32[]{:S(2)}, u32[]{:S(2)}) collective-permute-start(f32[2,128,128]{2,1,0:T(8,128)S(1)} %assemble.3.mid_ref), channel_id=1, source_target_pairs={{0,4},{2,6},{4,8},{5,1},{6,10},{7,3},{8,12},{9,5},{10,14},{11,7},{... | collective-permute-start | bytes 393224 | tf_op jit(solution)/shard_map/ppermute | solution.py:43
  24.8 1.9 %collective-permute-done.4.far_ref = f32[2,128,128]{2,1,0:T(8,128)S(1)} collective-permute-done((f32[2,128,128]{2,1,0:T(8,128)S(1)}, f32[2,128,128]{2,1,0:T(8,128)S(1)}, u32[]{:S(2)}, u32[]{:S(2)}) %collective-permute-start.4) | collective-permute-done | bytes 131104 | tf_op jit(solution)/shard_map/ppermute | solution.py:43
  26.8 1.9 %collective-permute-start.5 = (f32[2,128,128]{2,1,0:T(8,128)S(1)}, f32[2,128,128]{2,1,0:T(8,128)S(1)}, u32[]{:S(2)}, u32[]{:S(2)}) collective-permute-start(f32[2,128,128]{2,1,0:T(8,128)S(1)} %collective-permute-done.4.far_ref), channel_id=1, source_target_pairs={{0,1},{1,0},{2,3},{3,2},{4,5},{5,4},{6,7},{7,6},{8,9},{9,8},{10,11... | collective-permute-start | bytes 393224 | tf_op jit(solution)/shard_map/ppermute | solution.py:43
  28.6 0.0 copy-done
  28.6 6.0 %weights.1 = bf16[4,4,768,1152]{3,2,1,0:T(8,128)(2,1)S(1)} custom-call(f32[3,3,3,384,384]{4,3,2,1,0:T(8,128)S(1)} %copy-done), custom_call_target="tpu_custom_call" | custom-call | flops 4000000000 | bytes 262144 | tf_op jit(solution)/shard_map/weights/pallas_call | solution.py:265
  34.6 0.0 collective-permute-done.5.near_ref
  34.6 0.0 copy-done.3
  34.6 0.0 copy-done.5
  34.6 0.0 copy-done.6
  34.6 0.0 copy-done.7
  34.7 0.0 copy-done.8
  34.7 0.0 copy-start.1
  34.7 0.0 copy-start.2
  34.7 0.0 copy-start.4
  34.7 0.0 copy-start.9
  34.7 16.5 %blend.1 = (f32[2,384,384]{2,1,0:T(8,128)S(1)}, f32[384,384]{1,0:T(8,128)S(1)}) custom-call(f32[2,128,128]{2,1,0:T(8,128)S(1)} %assemble.3.mid_ref, f32[2,128,128]{2,1,0:T(8,128)S(1)} %collective-permute-done.4.far_ref, f32[2,128,128]{2,1,0:T(8,128)S(1)} %collective-permute-done.5.near_ref, f32[432,384]{1,0:T(8,128)S(1)} %bitcast.11, f32[384]{0:T(512)S(1)} %copy-done.5, ...), custom_call_target="tpu_custom_call" | custom-call | flops 1000000 | bytes 262144 | tf_op jit(solution)/shard_map/blend/pallas_call | solution.py:274
  51.2 0.1 collective-permute-start.6
  51.3 2.0 %collective-permute-done.6.got_ref = f32[384,384]{1,0:T(8,128)S(1)} collective-permute-done((f32[384,384]{1,0:T(8,128)S(1)}, f32[384,384]{1,0:T(8,128)S(1)}, u32[]{:S(2)}, u32[]{:S(2)}) %collective-permute-start.6) | collective-permute-done | bytes 589856 | tf_op jit(solution)/shard_map/ppermute | solution.py:43
  53.3 0.0 copy-done.1
  53.3 0.0 copy-done.2
  53.3 0.0 copy-done.4
  53.3 0.0 copy-done.9
  53.3 9.2 %upsample.1 = f32[2,8,192,128]{3,2,1,0:T(8,128)} custom-call(f32[2,384,384]{2,1,0:T(8,128)S(1)} %get-tuple-element.7.own_ref, f32[384,384]{1,0:T(8,128)S(1)} %collective-permute-done.6.got_ref, f32[1152,768]{1,0:T(8,128)S(1)} %bitcast.9, f32[768]{0:T(1024)S(1)} %copy-done.4, f32[3,3,192,384]{3,2,1,0:T(8,128)S(1)} %bitcast.10, f32[192]{0:T(256)S(1)} %copy-done.9), custom_call_target="tpu_custom_call" | custom-call | tf_op jit(solution)/shard_map/upsample/pallas_call | solution.py:296
  (2 shorter events, 0.0 us)
Async XLA Ops:
  0.0 1.7 %collective-permute-start = (f32[64,64]{1,0:T(8,128)}, f32[64,64]{1,0:T(8,128)S(1)}, u32[]{:S(2)}, u32[]{:S(2)}) collective-permute-start(f32[64,64]{1,0:T(8,128)} %bitcast.13), channel_id=1, source_target_pairs={{0,1},{1,0},{2,3},{3,2},{4,5},{5,4},{6,7},{7,6},{8,9},{9,8},{10,11... | collective-permute-start | bytes 49160 | tf_op jit(solution)/shard_map/ppermute | solution.py:43
  1.7 0.8 %copy-start.10 = (f32[1,4,16,1,64]{4,3,2,1,0:T(1,128)S(1)}, f32[1,4,16,1,64]{4,3,2,1,0:T(1,128)}, u32[]{:S(2)}) copy-start(f32[1,4,16,1,64]{4,3,2,1,0:T(1,128)} %param.11) | copy-start | bytes 49156
  2.6 4.3 %collective-permute-start.1 = (f32[64,128]{1,0:T(8,128)S(1)}, f32[64,128]{1,0:T(8,128)S(1)}, u32[]{:S(2)}, u32[]{:S(2)}) collective-permute-start(f32[64,128]{1,0:T(8,128)S(1)} %assemble.2), channel_id=1, source_target_pairs={{0,2},{1,3},{2,0},{3,1},{4,6},{5,7},{6,4},{7,5},{8,10},{9,11},{10,... | collective-permute-start | bytes 98312 | tf_op jit(solution)/shard_map/ppermute | solution.py:43
  6.9 5.0 %collective-permute-start.2 = (f32[2,64,128]{2,1,0:T(8,128)S(1)}, f32[2,64,128]{2,1,0:T(8,128)S(1)}, u32[]{:S(2)}, u32[]{:S(2)}) collective-permute-start(f32[2,64,128]{2,1,0:T(8,128)S(1)} %maximum_select_fusion.slab_ref), channel_id=1, source_target_pairs={{0,64},{1,33},{2,34},{3,35},{4,68},{5,37},{6,38},{7,39},{8,72},{9,... | collective-permute-start | bytes 196616 | tf_op jit(solution)/shard_map/ppermute | solution.py:43
  11.9 6.9 %collective-permute-start.3 = (f32[2,64,128]{2,1,0:T(8,128)S(1)}, f32[2,64,128]{2,1,0:T(8,128)S(1)}, u32[]{:S(2)}, u32[]{:S(2)}) collective-permute-start(f32[2,64,128]{2,1,0:T(8,128)S(1)} %collective-permute-done.2.before_ref), channel_id=1, source_target_pairs={{0,1},{1,0},{4,5},{5,4},{8,9},{9,8},{12,13},{13,12},{16,17},{17,16... | collective-permute-start | bytes 196616 | tf_op jit(solution)/shard_map/ppermute | solution.py:43
  18.8 9.8 %copy-start = (f32[3,3,3,384,384]{4,3,2,1,0:T(8,128)S(1)}, f32[3,3,3,384,384]{4,3,2,1,0:T(8,128)}, u32[]{:S(2)}) copy-start(f32[3,3,3,384,384]{4,3,2,1,0:T(8,128)} %raw.1) | copy-start | bytes 47775748
  18.9 15.8 %copy-start.3 = (f32[3,3,3,16,384]{4,3,2,1,0:T(8,128)S(1)}, f32[3,3,3,16,384]{4,3,2,1,0:T(8,128)}, u32[]{:S(2)}) copy-start(f32[3,3,3,16,384]{4,3,2,1,0:T(8,128)} %param.12) | copy-start | bytes 1990660
  18.9 15.8 %copy-start.5 = (f32[384]{0:T(512)S(1)}, f32[384]{0:T(512)}, u32[]{:S(2)}) copy-start(f32[384]{0:T(512)} %b_in_ref.1) | copy-start | bytes 4612
  18.9 15.8 %copy-start.6 = (f32[384]{0:T(512)S(1)}, f32[384]{0:T(512)}, u32[]{:S(2)}) copy-start(f32[384]{0:T(512)} %gain_ref.1) | copy-start | bytes 4612
  18.9 15.7 %copy-start.7 = (f32[384]{0:T(512)S(1)}, f32[384]{0:T(512)}, u32[]{:S(2)}) copy-start(f32[384]{0:T(512)} %shift_ref.1) | copy-start | bytes 4612
  18.9 15.7 %copy-start.8 = (f32[384]{0:T(512)S(1)}, f32[384]{0:T(512)}, u32[]{:S(2)}) copy-start(f32[384]{0:T(512)} %b_mid_ref.1) | copy-start | bytes 4612
  18.9 7.8 %collective-permute-start.4 = (f32[2,128,128]{2,1,0:T(8,128)S(1)}, f32[2,128,128]{2,1,0:T(8,128)S(1)}, u32[]{:S(2)}, u32[]{:S(2)}) collective-permute-start(f32[2,128,128]{2,1,0:T(8,128)S(1)} %assemble.3.mid_ref), channel_id=1, source_target_pairs={{0,4},{2,6},{4,8},{5,1},{6,10},{7,3},{8,12},{9,5},{10,14},{11,7},{... | collective-permute-start | bytes 393224 | tf_op jit(solution)/shard_map/ppermute | solution.py:43
  26.8 7.9 %collective-permute-start.5 = (f32[2,128,128]{2,1,0:T(8,128)S(1)}, f32[2,128,128]{2,1,0:T(8,128)S(1)}, u32[]{:S(2)}, u32[]{:S(2)}) collective-permute-start(f32[2,128,128]{2,1,0:T(8,128)S(1)} %collective-permute-done.4.far_ref), channel_id=1, source_target_pairs={{0,1},{1,0},{2,3},{3,2},{4,5},{5,4},{6,7},{7,6},{8,9},{9,8},{10,11... | collective-permute-start | bytes 393224 | tf_op jit(solution)/shard_map/ppermute | solution.py:43
  34.7 18.6 %copy-start.1 = (f32[3,384,768]{2,1,0:T(8,128)S(1)}, f32[3,384,768]{2,1,0:T(8,128)}, u32[]{:S(2)}) copy-start(f32[3,384,768]{2,1,0:T(8,128)} %param.18) | copy-start | bytes 10616836
  34.7 18.6 %copy-start.2 = (f32[3,3,384,192]{2,3,1,0:T(8,128)S(1)}, f32[3,3,384,192]{2,3,1,0:T(8,128)}, u32[]{:S(2)}) copy-start(f32[3,3,384,192]{2,3,1,0:T(8,128)} %param.20) | copy-start | bytes 7962628
  34.7 18.6 %copy-start.4 = (f32[768]{0:T(1024)S(1)}, f32[768]{0:T(1024)}, u32[]{:S(2)}) copy-start(f32[768]{0:T(1024)} %b_time_ref.1) | copy-start | bytes 9220
  34.7 18.6 %copy-start.9 = (f32[192]{0:T(256)S(1)}, f32[192]{0:T(256)}, u32[]{:S(2)}) copy-start(f32[192]{0:T(256)} %b_up_ref.1) | copy-start | bytes 2308
  51.2 2.1 %collective-permute-start.6 = (f32[384,384]{1,0:T(8,128)S(1)}, f32[384,384]{1,0:T(8,128)S(1)}, u32[]{:S(2)}, u32[]{:S(2)}) collective-permute-start(f32[384,384]{1,0:T(8,128)S(1)} %get-tuple-element.8), channel_id=1, source_target_pairs={{0,1},{1,0},{2,3},{3,2},{4,5},{5,4},{6,7},{7,6},{8,9},{9,8},{10,11... | collective-permute-start | bytes 1769480 | tf_op jit(solution)/shard_map/ppermute | solution.py:43

commit v3 on v2

--- a/solution.py
+++ b/solution.py
@@ -245,7 +245,7 @@
     )(*parts)
 
 
-def gather_latents(latents):
+def gather_latents(latents, w_mid):
     half = lax.axis_index("seq") // 2
     row = latents[0, :, :, 0, :].reshape(64, 64)
     other = send(row, lambda t, h, s: (t, h, s ^ 1))
@@ -256,12 +256,6 @@
     beside = send(before, lambda t, h, s: (t, h, s ^ 1) if s < 2 else None)
     frames = assemble(frames_kernel, (2, 128, 128), slab, before, beside)
     far = send(frames, lambda t, h, s: (t, h + 1 if s % 2 == 0 else h - 1, s))
-    near = send(far, lambda t, h, s: (t, h, s ^ 1))
-    return frames, far, near
-
-
-def body(latents, w_in, b_in, norm_gain, norm_shift, w_mid, b_mid, w_time, b_time, w_up, b_up):
-    frames, far, near = gather_latents(latents)
     weights = pl.pallas_call(
         weights_kernel,
         out_shape=jax.ShapeDtypeStruct((4, 4, 768, 1152), BF16),
@@ -271,6 +265,13 @@
         compiler_params=pltpu.CompilerParams(vmem_limit_bytes=1 << 20),
         name="weights",
     )(w_mid)
+    far, weights = lax.optimization_barrier((far, weights))
+    near = send(far, lambda t, h, s: (t, h, s ^ 1))
+    return frames, far, near, weights
+
+
+def body(latents, w_in, b_in, norm_gain, norm_shift, w_mid, b_mid, w_time, b_time, w_up, b_up):
+    frames, far, near, weights = gather_latents(latents, w_mid)
     own, outgoing = pl.pallas_call(
         blend_kernel,
         out_shape=(

time: 62.7 us -> 60.3 us (0.962)
  starting transfers between devices: 17.8 us -> 16.1 us
  waiting for transfers between devices: 12 us -> 11.3 us
    ppermute x7, starting transfers between devices: 17.8 us -> 16.1 us  [send(): return lax.ppermute(value, AXES, pairs)]
    ppermute x7, waiting for transfers between devices: 12 us -> 11.3 us  [send(): return lax.ppermute(value, AXES, pairs)]
where the time goes in v3:
time: 60.3 us; the launch traced here: 60.1 us
  Pallas kernels  31.7 us (53%)
  starting transfers between devices  16.1 us (27%)
  waiting for transfers between devices  11.3 us (19%)
  local copies, waits for them, and re-layouts  0.82 us (1%)
    pallas_call x1, Pallas kernels, body(): pl.pallas_call(blend_kernel, out_shape=(jax.ShapeDtypeStruct((2, 384, 384...  16.5 us
    ppermute x7, starting transfers between devices, send(): return lax.ppermute(value, AXES, pairs)  16.1 us
    ppermute x7, waiting for transfers between devices, send(): return lax.ppermute(value, AXES, pairs)  11.3 us
    pallas_call x1, Pallas kernels, body(): pl.pallas_call(upsample_kernel, out_shape=jax.ShapeDtypeStruct((2, 8, 192...  9.23 us
    pallas_call x1, Pallas kernels, gather_latents(): pl.pallas_call(weights_kernel, out_shape=jax.ShapeDtypeStruct((4, 4, 768,...  5.96 us
  transfers between devices with their start and end apart: 7, of which 6 were waited for; matrix products, arithmetic and copies ran while one was open for 0% of the time, Pallas kernels for 10%

profile of v3, /device:TPU:27, one launch (start us, length us, event | category | flops | bytes accessed | tf_op | source)
XLA Modules:
  0.0 60.1 jit_solution(6761437904017312846)
XLA Ops:
  0.0 0.7 %collective-permute-start = (f32[64,64]{1,0:T(8,128)}, f32[64,64]{1,0:T(8,128)S(1)}, u32[]{:S(2)}, u32[]{:S(2)}) collective-permute-start(f32[64,64]{1,0:T(8,128)} %bitcast.13), channel_id=1, source_target_pairs={{0,1},{1,0},{2,3},{3,2},{4,5},{5,4},{6,7},{7,6},{8,9},{9,8},{10,11... | collective-permute-start | bytes 49160 | tf_op jit(solution)/shard_map/ppermute | solution.py:43
  0.7 1.1 %collective-permute-done.other_ref = f32[64,64]{1,0:T(8,128)S(1)} collective-permute-done((f32[64,64]{1,0:T(8,128)}, f32[64,64]{1,0:T(8,128)S(1)}, u32[]{:S(2)}, u32[]{:S(2)}) %collective-permute-start) | collective-permute-done | bytes 16416 | tf_op jit(solution)/shard_map/ppermute | solution.py:43
  1.7 0.0 copy-start.10
  1.7 0.8 %copy-done.10 = f32[1,4,16,1,64]{4,3,2,1,0:T(1,128)S(1)} copy-done((f32[1,4,16,1,64]{4,3,2,1,0:T(1,128)S(1)}, f32[1,4,16,1,64]{4,3,2,1,0:T(1,128)}, u32[]{:S(2)}) %copy-start.10) | copy-done | bytes 16408
  2.5 0.1 assemble.2
  2.6 1.9 %collective-permute-start.1 = (f32[64,128]{1,0:T(8,128)S(1)}, f32[64,128]{1,0:T(8,128)S(1)}, u32[]{:S(2)}, u32[]{:S(2)}) collective-permute-start(f32[64,128]{1,0:T(8,128)S(1)} %assemble.2), channel_id=1, source_target_pairs={{0,2},{1,3},{2,0},{3,1},{4,6},{5,7},{6,4},{7,5},{8,10},{9,11},{10,... | collective-permute-start | bytes 98312 | tf_op jit(solution)/shard_map/ppermute | solution.py:43
  4.4 2.4 %collective-permute-done.1 = f32[64,128]{1,0:T(8,128)S(1)} collective-permute-done((f32[64,128]{1,0:T(8,128)S(1)}, f32[64,128]{1,0:T(8,128)S(1)}, u32[]{:S(2)}, u32[]{:S(2)}) %collective-permute-start.1) | collective-permute-done | bytes 32800 | tf_op jit(solution)/shard_map/ppermute | solution.py:43
  6.9 1.3 %collective-permute-start.2 = (f32[2,64,128]{2,1,0:T(8,128)S(1)}, f32[2,64,128]{2,1,0:T(8,128)S(1)}, u32[]{:S(2)}, u32[]{:S(2)}) collective-permute-start(f32[2,64,128]{2,1,0:T(8,128)S(1)} %maximum_select_fusion.slab_ref), channel_id=1, source_target_pairs={{0,64},{1,33},{2,34},{3,35},{4,68},{5,37},{6,38},{7,39},{8,72},{9,... | collective-permute-start | bytes 196616 | tf_op jit(solution)/shard_map/ppermute | solution.py:43
  8.2 3.7 %collective-permute-done.2.before_ref = f32[2,64,128]{2,1,0:T(8,128)S(1)} collective-permute-done((f32[2,64,128]{2,1,0:T(8,128)S(1)}, f32[2,64,128]{2,1,0:T(8,128)S(1)}, u32[]{:S(2)}, u32[]{:S(2)}) %collective-permute-start.2) | collective-permute-done | bytes 65568 | tf_op jit(solution)/shard_map/ppermute | solution.py:43
  11.9 6.0 %collective-permute-start.3 = (f32[2,64,128]{2,1,0:T(8,128)S(1)}, f32[2,64,128]{2,1,0:T(8,128)S(1)}, u32[]{:S(2)}, u32[]{:S(2)}) collective-permute-start(f32[2,64,128]{2,1,0:T(8,128)S(1)} %collective-permute-done.2.before_ref), channel_id=1, source_target_pairs={{0,1},{1,0},{4,5},{5,4},{8,9},{9,8},{12,13},{13,12},{16,17},{17,16... | collective-permute-start | bytes 196616 | tf_op jit(solution)/shard_map/ppermute | solution.py:43
  18.0 0.9 %collective-permute-done.3.beside_ref = f32[2,64,128]{2,1,0:T(8,128)S(1)} collective-permute-done((f32[2,64,128]{2,1,0:T(8,128)S(1)}, f32[2,64,128]{2,1,0:T(8,128)S(1)}, u32[]{:S(2)}, u32[]{:S(2)}) %collective-permute-start.3) | collective-permute-done | bytes 65568 | tf_op jit(solution)/shard_map/ppermute | solution.py:43
  18.8 0.0 copy-start
  18.9 0.0 copy-start.3
  18.9 0.0 copy-start.5
  18.9 0.0 copy-start.6
  18.9 0.0 copy-start.7
  18.9 0.0 copy-start.8
  18.9 5.9 %collective-permute-start.4 = (f32[2,128,128]{2,1,0:T(8,128)S(1)}, f32[2,128,128]{2,1,0:T(8,128)S(1)}, u32[]{:S(2)}, u32[]{:S(2)}) collective-permute-start(f32[2,128,128]{2,1,0:T(8,128)S(1)} %assemble.3.mid_ref), channel_id=1, source_target_pairs={{0,4},{2,6},{4,8},{5,1},{6,10},{7,3},{8,12},{9,5},{10,14},{11,7},{... | collective-permute-start | bytes 393224 | tf_op jit(solution)/shard_map/ppermute | solution.py:43
  24.8 0.0 copy-done
  24.8 6.0 %weights.1 = bf16[4,4,768,1152]{3,2,1,0:T(8,128)(2,1)S(1)} custom-call(f32[3,3,3,384,384]{4,3,2,1,0:T(8,128)S(1)} %copy-done), custom_call_target="tpu_custom_call" | custom-call | flops 4000000000 | bytes 262144 | tf_op jit(solution)/shard_map/weights/pallas_call | solution.py:259
  30.8 0.0 collective-permute-done.4.far_ref
  30.8 0.1 collective-permute-start.5
  30.9 1.3 %collective-permute-done.5.near_ref = f32[2,128,128]{2,1,0:T(8,128)S(1)} collective-permute-done((f32[2,128,128]{2,1,0:T(8,128)S(1)}, f32[2,128,128]{2,1,0:T(8,128)S(1)}, u32[]{:S(2)}, u32[]{:S(2)}) %collective-permute-start.5) | collective-permute-done | bytes 131104 | tf_op jit(solution)/shard_map/ppermute | solution.py:43
  32.2 0.0 copy-done.3
  32.2 0.0 copy-done.5
  32.2 0.0 copy-done.6
  32.3 0.0 copy-done.7
  32.3 0.0 copy-done.8
  32.3 0.0 copy-start.1
  32.3 0.0 copy-start.2
  32.3 0.0 copy-start.4
  32.3 0.0 copy-start.9
  32.3 16.5 %blend.1 = (f32[2,384,384]{2,1,0:T(8,128)S(1)}, f32[384,384]{1,0:T(8,128)S(1)}) custom-call(f32[2,128,128]{2,1,0:T(8,128)S(1)} %assemble.3.mid_ref, f32[2,128,128]{2,1,0:T(8,128)S(1)} %collective-permute-done.4.far_ref, f32[2,128,128]{2,1,0:T(8,128)S(1)} %collective-permute-done.5.near_ref, f32[432,384]{1,0:T(8,128)S(1)} %bitcast.11, f32[384]{0:T(512)S(1)} %copy-done.5, ...), custom_call_target="tpu_custom_call" | custom-call | flops 1000000 | bytes 262144 | tf_op jit(solution)/shard_map/blend/pallas_call | solution.py:275
  48.8 0.2 collective-permute-start.6
  49.0 1.8 %collective-permute-done.6.got_ref = f32[384,384]{1,0:T(8,128)S(1)} collective-permute-done((f32[384,384]{1,0:T(8,128)S(1)}, f32[384,384]{1,0:T(8,128)S(1)}, u32[]{:S(2)}, u32[]{:S(2)}) %collective-permute-start.6) | collective-permute-done | bytes 589856 | tf_op jit(solution)/shard_map/ppermute | solution.py:43
  50.9 0.0 copy-done.1
  50.9 0.0 copy-done.2
  50.9 0.0 copy-done.4
  50.9 0.0 copy-done.9
  50.9 9.2 %upsample.1 = f32[2,8,192,128]{3,2,1,0:T(8,128)} custom-call(f32[2,384,384]{2,1,0:T(8,128)S(1)} %get-tuple-element.11.own_ref, f32[384,384]{1,0:T(8,128)S(1)} %collective-permute-done.6.got_ref, f32[1152,768]{1,0:T(8,128)S(1)} %bitcast.9, f32[768]{0:T(1024)S(1)} %copy-done.4, f32[3,3,192,384]{3,2,1,0:T(8,128)S(1)} %bitcast.10, f32[192]{0:T(256)S(1)} %copy-done.9), custom_call_target="tpu_custom_call" | custom-call | tf_op jit(solution)/shard_map/upsample/pallas_call | solution.py:297
  (2 shorter events, 0.0 us)
Async XLA Ops:
  0.0 1.7 %collective-permute-start = (f32[64,64]{1,0:T(8,128)}, f32[64,64]{1,0:T(8,128)S(1)}, u32[]{:S(2)}, u32[]{:S(2)}) collective-permute-start(f32[64,64]{1,0:T(8,128)} %bitcast.13), channel_id=1, source_target_pairs={{0,1},{1,0},{2,3},{3,2},{4,5},{5,4},{6,7},{7,6},{8,9},{9,8},{10,11... | collective-permute-start | bytes 49160 | tf_op jit(solution)/shard_map/ppermute | solution.py:43
  1.7 0.8 %copy-start.10 = (f32[1,4,16,1,64]{4,3,2,1,0:T(1,128)S(1)}, f32[1,4,16,1,64]{4,3,2,1,0:T(1,128)}, u32[]{:S(2)}) copy-start(f32[1,4,16,1,64]{4,3,2,1,0:T(1,128)} %param.11) | copy-start | bytes 49156
  2.6 4.3 %collective-permute-start.1 = (f32[64,128]{1,0:T(8,128)S(1)}, f32[64,128]{1,0:T(8,128)S(1)}, u32[]{:S(2)}, u32[]{:S(2)}) collective-permute-start(f32[64,128]{1,0:T(8,128)S(1)} %assemble.2), channel_id=1, source_target_pairs={{0,2},{1,3},{2,0},{3,1},{4,6},{5,7},{6,4},{7,5},{8,10},{9,11},{10,... | collective-permute-start | bytes 98312 | tf_op jit(solution)/shard_map/ppermute | solution.py:43
  6.9 5.0 %collective-permute-start.2 = (f32[2,64,128]{2,1,0:T(8,128)S(1)}, f32[2,64,128]{2,1,0:T(8,128)S(1)}, u32[]{:S(2)}, u32[]{:S(2)}) collective-permute-start(f32[2,64,128]{2,1,0:T(8,128)S(1)} %maximum_select_fusion.slab_ref), channel_id=1, source_target_pairs={{0,64},{1,33},{2,34},{3,35},{4,68},{5,37},{6,38},{7,39},{8,72},{9,... | collective-permute-start | bytes 196616 | tf_op jit(solution)/shard_map/ppermute | solution.py:43
  11.9 6.9 %collective-permute-start.3 = (f32[2,64,128]{2,1,0:T(8,128)S(1)}, f32[2,64,128]{2,1,0:T(8,128)S(1)}, u32[]{:S(2)}, u32[]{:S(2)}) collective-permute-start(f32[2,64,128]{2,1,0:T(8,128)S(1)} %collective-permute-done.2.before_ref), channel_id=1, source_target_pairs={{0,1},{1,0},{4,5},{5,4},{8,9},{9,8},{12,13},{13,12},{16,17},{17,16... | collective-permute-start | bytes 196616 | tf_op jit(solution)/shard_map/ppermute | solution.py:43
  18.8 6.0 %copy-start = (f32[3,3,3,384,384]{4,3,2,1,0:T(8,128)S(1)}, f32[3,3,3,384,384]{4,3,2,1,0:T(8,128)}, u32[]{:S(2)}) copy-start(f32[3,3,3,384,384]{4,3,2,1,0:T(8,128)} %raw.1) | copy-start | bytes 47775748
  18.9 13.4 %copy-start.3 = (f32[3,3,3,16,384]{4,3,2,1,0:T(8,128)S(1)}, f32[3,3,3,16,384]{4,3,2,1,0:T(8,128)}, u32[]{:S(2)}) copy-start(f32[3,3,3,16,384]{4,3,2,1,0:T(8,128)} %param.12) | copy-start | bytes 1990660
  18.9 13.4 %copy-start.5 = (f32[384]{0:T(512)S(1)}, f32[384]{0:T(512)}, u32[]{:S(2)}) copy-start(f32[384]{0:T(512)} %b_in_ref.1) | copy-start | bytes 4612
  18.9 13.4 %copy-start.6 = (f32[384]{0:T(512)S(1)}, f32[384]{0:T(512)}, u32[]{:S(2)}) copy-start(f32[384]{0:T(512)} %gain_ref.1) | copy-start | bytes 4612
  18.9 13.4 %copy-start.7 = (f32[384]{0:T(512)S(1)}, f32[384]{0:T(512)}, u32[]{:S(2)}) copy-start(f32[384]{0:T(512)} %shift_ref.1) | copy-start | bytes 4612
  18.9 13.4 %copy-start.8 = (f32[384]{0:T(512)S(1)}, f32[384]{0:T(512)}, u32[]{:S(2)}) copy-start(f32[384]{0:T(512)} %b_mid_ref.1) | copy-start | bytes 4612
  18.9 11.9 %collective-permute-start.4 = (f32[2,128,128]{2,1,0:T(8,128)S(1)}, f32[2,128,128]{2,1,0:T(8,128)S(1)}, u32[]{:S(2)}, u32[]{:S(2)}) collective-permute-start(f32[2,128,128]{2,1,0:T(8,128)S(1)} %assemble.3.mid_ref), channel_id=1, source_target_pairs={{0,4},{2,6},{4,8},{5,1},{6,10},{7,3},{8,12},{9,5},{10,14},{11,7},{... | collective-permute-start | bytes 393224 | tf_op jit(solution)/shard_map/ppermute | solution.py:43
  30.8 1.4 %collective-permute-start.5 = (f32[2,128,128]{2,1,0:T(8,128)S(1)}, f32[2,128,128]{2,1,0:T(8,128)S(1)}, u32[]{:S(2)}, u32[]{:S(2)}) collective-permute-start(f32[2,128,128]{2,1,0:T(8,128)S(1)} %collective-permute-done.4.far_ref), channel_id=1, source_target_pairs={{0,1},{1,0},{2,3},{3,2},{4,5},{5,4},{6,7},{7,6},{8,9},{9,8},{10,11... | collective-permute-start | bytes 393224 | tf_op jit(solution)/shard_map/ppermute | solution.py:43
  32.3 18.6 %copy-start.1 = (f32[3,384,768]{2,1,0:T(8,128)S(1)}, f32[3,384,768]{2,1,0:T(8,128)}, u32[]{:S(2)}) copy-start(f32[3,384,768]{2,1,0:T(8,128)} %param.18) | copy-start | bytes 10616836
  32.3 18.6 %copy-start.2 = (f32[3,3,384,192]{2,3,1,0:T(8,128)S(1)}, f32[3,3,384,192]{2,3,1,0:T(8,128)}, u32[]{:S(2)}) copy-start(f32[3,3,384,192]{2,3,1,0:T(8,128)} %param.20) | copy-start | bytes 7962628
  32.3 18.6 %copy-start.4 = (f32[768]{0:T(1024)S(1)}, f32[768]{0:T(1024)}, u32[]{:S(2)}) copy-start(f32[768]{0:T(1024)} %b_time_ref.1) | copy-start | bytes 9220
  32.3 18.6 %copy-start.9 = (f32[192]{0:T(256)S(1)}, f32[192]{0:T(256)}, u32[]{:S(2)}) copy-start(f32[192]{0:T(256)} %b_up_ref.1) | copy-start | bytes 2308
  48.8 2.1 %collective-permute-start.6 = (f32[384,384]{1,0:T(8,128)S(1)}, f32[384,384]{1,0:T(8,128)S(1)}, u32[]{:S(2)}, u32[]{:S(2)}) collective-permute-start(f32[384,384]{1,0:T(8,128)S(1)} %get-tuple-element.12), channel_id=1, source_target_pairs={{0,1},{1,0},{2,3},{3,2},{4,5},{5,4},{6,7},{7,6},{8,9},{9,8},{10,11... | collective-permute-start | bytes 1769480 | tf_op jit(solution)/shard_map/ppermute | solution.py:43
